TPU v7x, 32 devices: a whole 2x2x4 slice. The times are simulated.
32 devices in a mesh: section: 2 (over core), dp: 16 (over z, y, x).
Axes of the slice: x: 2, y: 2, z: 4, core: 2. Of those that a mesh axis runs over, the one named last changes fastest.
Arguments:
- section_inputs: bfloat16 [2, 2, 16384, 800], P('section', None, 'dp'), may hold values from -6 to 6
- seq_lengths: int32 [2, 128], P(None, 'dp'), may hold values from 0 to 1024, as said below
- dilations: int32 [2], P('section'), may hold values from 1 to 16, as said below
- gains_in: float32 [2, 800], P('section'), may hold values from 0.5 to 1.5
- biases_in: float32 [2, 800], P('section'), may hold values from -1.5 to 1.5
- gains_mid: float32 [2, 2, 400], P('section'), may hold values from 0.5 to 1.5
- biases_mid: float32 [2, 2, 400], P('section'), may hold values from -1.5 to 1.5
- out_bias: float32 [2, 800], P('section'), may hold values from -1.5 to 1.5
- w_in: bfloat16 [2, 800, 400], P('section'), may hold values from -0.21875 to 0.21875
- w_out: bfloat16 [2, 400, 800], P('section'), may hold values from -0.625 to 0.625
- conv_taps: bfloat16 [2, 5, 400, 400], P('section'), may hold values from -0.125 to 0.125
Outputs:
- block_out: bfloat16 [2, 2, 16384, 800], P('section', None, 'dp')
- input_grad: bfloat16 [2, 2, 16384, 800], P('section', None, 'dp')
- grad_gains_in: float32 [2, 800], P('section')
- grad_biases_in: float32 [2, 800], P('section')
- grad_gains_mid: float32 [2, 2, 400], P('section')
- grad_biases_mid: float32 [2, 2, 400], P('section')
- grad_out_bias: float32 [2, 800], P('section')
- grad_w_in: float32 [2, 800, 400], P('section')
- grad_w_out: float32 [2, 400, 800], P('section')
- grad_conv_taps: float32 [2, 5, 400, 400], P('section')
Inputs may be any that keep to these rules, and one draw needn't show every extreme that they name: `seq_lengths`: each index of dp holds, in each micro-batch, 1024 tokens made of whole sequences of 128, 256, 512 or 1024 tokens, each beginning at a multiple of its own length within those tokens; an entry is the length of the sequence that begins at that unit, 0 where none begins; some index holds one sequence of 1024 tokens. `dilations`: powers of two; one of the two is 16.
All inputs are finite; a program needn't handle non-finite values.
Results may differ from a plain program's by a relative error of at most 0.012.
Values may be sent and summed in bfloat16 or wider, within the bound.
No kernel may reach another device: no remote copies, remote signals or barrier semaphores. Data moves between devices by JAX's collectives and lax.ppermute only.
A program may use at most 192 MiB of HBM per device.

v0:
```python
import functools

import jax
import jax.numpy as jnp
from jax import lax
from jax.experimental import pallas as pl
from jax.experimental.pallas import tpu as pltpu
from jax.sharding import PartitionSpec as P

DEC_TAPS = 3
EPS = 1e-05
LANES = 128
CHUNK = 80
VEC_ROWS = 48
SMALL_ROWS = 8
PIECES = 5
LOOPS = (False, False, True)
BF = jnp.bfloat16
F32 = jnp.float32
VMEM_LIMIT = 62 * 2**20
SMALL_LIMIT = 62 * 2**20
SEQ = "ddeedeyxdede"
ANY = pl.BlockSpec(memory_space=pl.ANY)
SMEM = pl.BlockSpec(memory_space=pltpu.SMEM)
VMEM = pl.BlockSpec(memory_space=pltpu.VMEM)


def shape(dims, dtype):
    return jax.ShapeDtypeStruct(tuple(dims), dtype)


def nn(left, right):
    return jnp.dot(left, right, preferred_element_type=F32)


def nt(left, right):
    return lax.dot_general(left, right, (((1,), (1,)), ((), ())), preferred_element_type=F32)


def tn(left, right):
    return lax.dot_general(left, right, (((0,), (0,)), ((), ())), preferred_element_type=F32)


def lane_block(index):
    return pl.ds(pl.multiple_of(index * LANES, LANES), LANES)


def chunks(rows):
    size = CHUNK if rows % CHUNK == 0 else 16
    return [slice(at, at + size) for at in range(0, rows, size)]


def folded(values):
    return jnp.sum(values.reshape(values.shape[0] // 8, 8, values.shape[1]), 0)


def column(vector):
    return jnp.broadcast_to(vector, (LANES, vector.shape[1])).T


def norm_forward(source, half_gain, half_bias, normed, slope, hidden, devs, row, units):
    feats, tokens = source.shape
    scale = 1.0 / feats

    def stats(here):
        base = source[0:1, here].astype(F32)
        total = jnp.zeros((8, LANES), F32)
        squares = jnp.zeros((8, LANES), F32)
        for part in chunks(feats):
            moved = source[part, here].astype(F32) - base
            total = total + folded(moved)
            squares = squares + folded(moved * moved)
        average = jnp.sum(total, 0, keepdims=True) * scale
        variance = jnp.sum(squares, 0, keepdims=True) * scale - average * average
        inverse_dev = lax.rsqrt(jnp.maximum(variance, 0.0) + EPS)
        return (average + base) * inverse_dev, inverse_dev

    def finish(here, offset, inverse_dev):
        devs[row : row + 1, here] = inverse_dev
        for part in chunks(feats):
            values = source[part, here].astype(F32) * inverse_dev - offset
            gain = half_gain[part, :]
            half = values * gain + half_bias[part, :]
            tan = jnp.tanh(half)
            weight = 1.0 + tan
            out = half * weight
            normed[part, here] = values.astype(BF)
            slope[part, here] = ((weight + out * (1.0 - tan)) * gain).astype(BF)
            hidden[part, here] = out.astype(hidden.dtype)

    if units is None:

        def body(unit, carry):
            following = stats(lane_block(jnp.minimum(unit + 1, tokens // LANES - 1)))
            finish(lane_block(unit), *carry)
            return following

        lax.fori_loop(0, tokens // LANES, body, stats(lane_block(0)))
        return
    for unit in units:
        here = slice(unit * LANES, (unit + 1) * LANES)
        finish(here, *stats(here))


def norm_backward(gradient, slope, normed, devs, row, gain_sums, bias_sums, means, emit, loops):
    feats, tokens = gradient.shape
    units = tokens // LANES
    scale = 1.0 / feats
    means[...] = jnp.zeros_like(means)

    def collect(rows, size):
        gain_sum = jnp.zeros((size, LANES), F32)
        bias_sum = jnp.zeros((size, LANES), F32)
        for unit in range(units):
            here = slice(unit * LANES, (unit + 1) * LANES)
            scaled = gradient[rows, here] * slope[rows, here].astype(F32)
            weighted = scaled * normed[rows, here].astype(F32)
            gain_sum = gain_sum + weighted
            bias_sum = bias_sum + scaled
            means[0:8, here] += folded(scaled)
            means[8:16, here] += folded(weighted)
        gain_sums[rows, :] = gain_sum
        bias_sums[rows, :] = bias_sum

    def finish(here):
        inverse_dev = devs[row : row + 1, here]
        first = jnp.sum(means[0:8, here], 0, keepdims=True) * (scale * inverse_dev)
        second = jnp.sum(means[8:16, here], 0, keepdims=True) * (scale * inverse_dev)
        for part in chunks(feats):
            scaled = gradient[part, here] * slope[part, here].astype(F32)
            emit(part, here, scaled * inverse_dev - first - normed[part, here].astype(F32) * second)

    if loops:
        size = chunks(feats)[0].stop

        def one_chunk(index, _):
            collect(pl.ds(pl.multiple_of(index * size, 16), size), size)
            return 0

        def one_unit(unit, _):
            finish(lane_block(unit))
            return 0

        lax.fori_loop(0, feats // size, one_chunk, 0)
        lax.fori_loop(0, units, one_unit, 0, unroll=2)
        return
    for part in chunks(feats):
        collect(part, part.stop - part.start)
    for unit in range(units):
        finish(slice(unit * LANES, (unit + 1) * LANES))


def write_shifts(source, target, begins, offsets, units):
    feats, tokens = source.shape
    count = tokens // LANES
    block = lambda unit: slice(unit * LANES, (unit + 1) * LANES)
    for unit in units:
        joined_behind = (begins(unit) == 0).astype(F32) if unit > 0 else None
        joined_ahead = (begins(unit + 1) == 0).astype(F32) if unit < count - 1 else None
        for part in chunks(feats):
            size = part.stop - part.start
            lane = lax.broadcasted_iota(jnp.int32, (size, LANES), 1)
            zero = jnp.zeros((size, LANES), F32)
            current = source[part, block(unit)].astype(F32)
            behind = zero if unit == 0 else source[part, block(unit - 1)].astype(F32) * joined_behind
            ahead = zero if unit == count - 1 else source[part, block(unit + 1)].astype(F32) * joined_ahead
            for position, (sign, step) in enumerate(offsets):
                if sign == 0:
                    moved = current
                elif sign < 0:
                    moved = pltpu.roll(jnp.where(lane < LANES - step, current, behind), step, 1)
                else:
                    moved = pltpu.roll(jnp.where(lane >= step, current, ahead), LANES - step, 1)
                rows = slice(feats * position + part.start, feats * position + part.stop)
                target[rows, block(unit)] = moved.astype(BF)


def tap_offsets(taps, dilation, flip):
    result = []
    for position in range(taps):
        factor = (position - 2) * (-1 if flip else 1)
        result.append(((factor > 0) - (factor < 0), abs(factor) * dilation))
    return result


def layout(taps, width, inner):
    wide = pl.cdiv(width, LANES) * inner
    taps_at = wide
    tails_at = taps_at + taps * (inner // LANES) * inner
    w_in_at = tails_at + inner
    vec_at = w_in_at + wide
    return taps_at, tails_at, w_in_at, vec_at, vec_at + VEC_ROWS


def scatter_groups(count, full):
    total = count.bit_length() - 1
    rest = [list(range(2, min(4, total)))] if full and total > 2 else []
    return [[[bit] for bit in bits if bit < total] + rest for bits in ((0, 1), (1, 0))]


def share_count(groups):
    return 2 ** sum(len(bits) for bits in groups)


def padded_rows(rows, groups):
    unit = 2 * 16 * share_count(groups[0])
    return pl.cdiv(rows, unit) * unit


def put_slabs(buf, row, matrix):
    rows, cols = matrix.shape
    for q in range(pl.cdiv(cols, LANES)):
        part = matrix[:, LANES * q : min(cols, LANES * (q + 1))]
        if part.shape[1] < LANES:
            part = jnp.concatenate([part, jnp.zeros((rows, LANES - part.shape[1]), F32)], 1)
        buf[row + q * rows : row + (q + 1) * rows, :] = part.astype(BF)


def put_taps(buf, taps, width, shifted, grad_mixed):
    inner = grad_mixed.shape[0]
    taps_at, tails_at, _, _, _ = layout(taps, width, inner)
    whole = inner // LANES
    tail = inner - whole * LANES
    for k in range(taps):
        grad = nt(shifted[inner * k : inner * (k + 1), :], grad_mixed[...])
        for q in range(whole):
            at = taps_at + inner * (whole * k + q)
            buf[at : at + inner, :] = grad[:, LANES * q : LANES * (q + 1)].astype(BF)
        buf[tails_at : tails_at + inner, tail * k : tail * (k + 1)] = grad[:, LANES * whole :].astype(BF)
    buf[tails_at : tails_at + inner, tail * taps :] = jnp.zeros((inner, LANES - tail * taps), BF)


def row_sums(acc):
    return jnp.sum(acc.T, 0, keepdims=True)


def put_vectors(buf, at, vec, sums):
    vec[...] = jnp.zeros_like(vec)
    row = 0
    for total in sums:
        for lane in range(0, total.shape[1], LANES):
            part = total[:, lane : lane + LANES]
            vec[row : row + 1, 0 : part.shape[1]] = part
            row += 1
    buf[at : at + VEC_ROWS, :] = vec[...].astype(BF)


def relative_index(position, groups):
    result = 0
    for bits in reversed(groups):
        size = 2 ** len(bits)
        result = result + (position & (size - 1)) * 2 ** bits[0]
        position = position >> len(bits)
    return result


def owner_of(position, side, groups, index):
    both = [relative_index(position, order) for order in groups]
    mask = sum(2**bit for bits in groups[0] for bit in bits)
    return jnp.where(side == 0, both[0], both[1]) ^ (index & mask)


def position_of(owner, side, groups, index):
    distance = owner ^ index
    position = 0
    for bits in groups[side]:
        position = position * 2 ** len(bits) + ((distance >> bits[0]) & (2 ** len(bits) - 1))
    return position


class RowsOut:
    def __init__(self, buf, keep, send, section, index, groups, sems):
        self.buf, self.keep, self.send, self.sems = buf, keep, send, sems
        self.section, self.index, self.groups = section, index, groups
        self.count = share_count(groups[0])
        self.share = keep.shape[0] // self.count
        self.sizes = []

    def start(self, first, last):
        for number in range(2 * self.count):
            low, high = max(first, number * self.share), min(last, (number + 1) * self.share)
            if low >= high:
                continue
            side, owner = divmod(number, self.count)
            place = position_of(owner, side, self.groups, self.index) * self.share + (low - number * self.share)
            target = pl.ds(pl.multiple_of(place, 16), high - low)
            source = self.buf.at[low:high]
            sem = self.sems.at[len(self.sizes)]
            pl.when(self.section == side)(pltpu.make_async_copy(source, self.keep.at[target], sem).start)
            pl.when(self.section != side)(pltpu.make_async_copy(source, self.send.at[target], sem).start)
            self.sizes.append(high - low)

    def wait(self):
        for number, size in enumerate(self.sizes):
            source, target = self.buf.at[0:size], self.keep.at[0:size]
            pltpu.make_async_copy(source, target, self.sems.at[number]).wait()


def forward_block(taps, begins, dilation, x, y, weights, turned, cols, kept, hmid, prod, ready):
    w_in_t, w_out, conv = weights
    w_out_t, conv_t = turned
    g1, b1, g2, b2, g3, b3, ob = cols
    n1, s1, r, n2, s2, n3, s3, hin, shifted, hout = kept
    inner, tokens = hmid.shape
    units = tokens // LANES
    narrow = prod.at[0:inner]
    parts = [range(at, min(at + units // 2, units)) for at in range(0, units, units // 2)]
    columns = [slice(part.start * LANES, part.stop * LANES) for part in parts]
    offsets = tap_offsets(taps, dilation, False)

    def mix(part):
        narrow[:, columns[part]] = nn(conv_t[:, 0 : taps * inner], shifted[:, columns[part]])

    def leave(part):
        here = columns[part]
        bias = jnp.concatenate([ob[...]] * len(parts[part]), 1)
        y[:, here] = (x[:, here].astype(F32) + nn(w_out_t[...], hout[:, here]) + bias).astype(BF)

    norm_forward(x, g1, b1, n1, s1, hin, r, 0, None)
    ready(0)
    narrow[...] = nn(w_in_t[...], hin[...])
    ready(1)
    norm_forward(narrow, g2, b2, n2, s2, hmid, r, 1, parts[0])
    for k in range(taps):
        conv_t[:, inner * k : inner * (k + 1)] = conv[k].T
    w_out_t[...] = w_out[...].T
    norm_forward(narrow, g2, b2, n2, s2, hmid, r, 1, parts[1])
    write_shifts(hmid, shifted, begins, offsets, parts[0])
    mix(0)
    write_shifts(hmid, shifted, begins, offsets, parts[1])
    mix(1)
    norm_forward(narrow, g3, b3, n3, s3, hout, r, 2, parts[0])
    leave(0)
    norm_forward(narrow, g3, b3, n3, s3, hout, r, 2, parts[1])
    leave(1)


def fill_columns(small, cols):
    g1, b1, g2, b2, g3, b3, ob = cols
    width, inner = g1.shape[0], g2.shape[0]
    for target, row, scale in ((g1, 0, 0.5), (b1, 1, 0.5), (ob, 2, 1.0)):
        target[...] = column(small[row : row + 1, 0:width] * scale)
    for target, row in ((g2, 3), (b2, 4), (g3, 5), (b3, 6)):
        target[...] = column(small[row : row + 1, 0:inner] * 0.5)


def back_third(gy, w_out, kept, prod, means, grad_mixed, gain_sums, bias_sums, beside):
    n3, s3, r = kept
    inner = w_out.shape[0]
    narrow = prod.at[0:inner]
    narrow[...] = nn(w_out[...], gy[...])
    beside()

    def emit(part, here, value):
        grad_mixed[part, here] = value.astype(BF)

    norm_backward(narrow, s3, n3, r, 2, gain_sums, bias_sums, means, emit, LOOPS[0])


def back_second(
    taps, begins, dilation, conv_w, kept, prod, means, grad_mixed, moved, grad_projected, gain_sums, bias_sums, ready,
    weights=None,
):
    n2, s2, r = kept
    inner = grad_mixed.shape[0]
    narrow = prod.at[0:inner]
    write_shifts(grad_mixed, moved, begins, tap_offsets(taps, dilation, True), range(grad_mixed.shape[1] // LANES))
    if weights is not None:
        weights()
    narrow[...] = nn(conv_w[...], moved[...])
    ready()

    def emit(part, here, value):
        grad_projected[part, here] = value.astype(BF)

    norm_backward(narrow, s2, n2, r, 1, gain_sums, bias_sums, means, emit, LOOPS[1])


def back_first(gy, w_in_t, kept, prod, means, grad_projected, gx, gain_sums, bias_sums, ready):
    n1, s1, r = kept
    prod[...] = tn(w_in_t[...], grad_projected[...])
    ready()

    def emit(part, here, value):
        gx[part, here] = (gy[part, here].astype(F32) + value).astype(BF)

    norm_backward(prod, s1, n1, r, 0, gain_sums, bias_sums, means, emit, LOOPS[2])


def put_w_out(buf, hout_ones, gy):
    grad = nt(hout_ones[...], gy[...])
    inner = hout_ones.shape[0] - 16
    put_slabs(buf, 0, grad[0:inner])
    return grad[inner : inner + 1]


def gain_and_bias(gain, sums):
    return [row_sums(acc[...]) / gain for acc in sums]


def put_rows(target, rows):
    target[...] = jnp.zeros_like(target)
    for at, row in enumerate(rows):
        target[at : at + 1, 0 : row.shape[1]] = row


def gains_of(small, width, inner):
    return small[0:1, 0:width], small[3:4, 0:inner], small[5:6, 0:inner]


def pick_small(leading, own, got):
    flag = leading.astype(F32)
    return own[...] * flag + got[...] * (1.0 - flag)


def start_all(copies):
    for copy in copies:
        copy.start()


def pick_rows_kernel(rows, send, hold, sem):
    section = lax.axis_index("section")
    size = send.shape[0] // PIECES
    parts = [slice(size * i, size * (i + 1)) for i in range(PIECES)]
    arrive = [
        pltpu.make_async_copy(rows.at[1 - section, part], hold.at[part], sem.at[i]) for i, part in enumerate(parts)
    ]
    leave = [pltpu.make_async_copy(hold.at[part], send.at[part], sem.at[PIECES + i]) for i, part in enumerate(parts)]
    start_all(arrive)
    for come, go in zip(arrive, leave):
        come.wait()
        go.start()
    for go in leave:
        go.wait()


def pick_rows(rows):
    return pl.pallas_call(
        pick_rows_kernel,
        in_specs=[ANY],
        out_specs=ANY,
        out_shape=shape(rows.shape[1:], BF),
        scratch_shapes=[pltpu.VMEM(rows.shape[1:], BF), pltpu.SemaphoreType.DMA((2 * PIECES,))],
        compiler_params=pltpu.CompilerParams(vmem_limit_bytes=VMEM_LIMIT),
        cost_estimate=pl.CostEstimate(flops=0, bytes_accessed=8 * 2**20, transcendentals=0),
        name="pick_rows",
    )(rows)


def pack_small_kernel(gin, bin_, gmid, bmid, out_bias, dilation, small):
    width, inner = gin.shape[1], gmid.shape[1]
    small[...] = jnp.zeros_like(small)
    for row, ref in ((0, gin), (1, bin_), (2, out_bias)):
        small[row : row + 1, 0:width] = ref[...]
    for row, ref, which in ((3, gmid, 0), (4, bmid, 0), (5, gmid, 1), (6, bmid, 1)):
        small[row : row + 1, 0:inner] = ref[which : which + 1, :]
    small[7:8, :] = jnp.full((1, small.shape[1]), dilation[0].astype(F32), F32)


def pack_small(gin, bin_, gmid, bmid, out_bias, dilation):
    return pl.pallas_call(
        pack_small_kernel,
        in_specs=[VMEM] * 5 + [SMEM],
        out_specs=VMEM,
        out_shape=shape((SMALL_ROWS, gin.shape[1]), F32),
        compiler_params=pltpu.CompilerParams(vmem_limit_bytes=VMEM_LIMIT),
        name="pack_small",
    )(gin, bin_, gmid, bmid, out_bias, dilation)


def kept_shapes(taps, width, inner, tokens):
    wide, narrow = (width, tokens), (inner, tokens)
    return [
        (wide, BF), (wide, BF), ((8, tokens), F32), (narrow, BF), (narrow, BF), (narrow, BF), (narrow, BF),
        (wide, BF), ((inner * taps, tokens), BF), (narrow, BF),
    ]


def column_shapes(width, inner):
    return [(width, LANES)] * 2 + [(inner, LANES)] * 4 + [(width, LANES)]


def main_kernel(taps_of, groups, *refs):
    refs = list(refs)

    def take(number):
        taken = refs[:number]
        del refs[:number]
        return taken

    seq, rows, got, small_own, small_got = take(5)
    own_w, got_w = take(3), take(3)
    outs, send_y, grad_out, keep_buf, send_buf, vec_out = take(6)
    kept_out = take(10)
    x, cot = take(2)
    enc_w, dec_w = take(3), take(3)
    small = take(2)
    enc_kept, dec_kept = take(10), take(10)
    cols = take(7)
    hmid, prod, means, y_enc, gx, w_out_t, conv_t, conv_w, grad_mixed, grad_projected, moved, buf = take(12)
    ag1, ab1, ag2, ab2, ag3, ab3, vec, sem, row_sems = take(9)

    section = lax.axis_index("section")
    index = lax.axis_index("dp")
    leading = section == 0
    width, tokens = x.shape
    inner = hmid.shape[0]
    small[0][...] = pick_small(leading, small_own, small_got)
    small[1][...] = pick_small(leading, small_got, small_own)
    dilation = [jnp.max(member[7:8, 0:LANES]).astype(jnp.int32) for member in small]

    def begins(unit):
        return seq[section, unit]

    loads = [(x, rows.at[0], got), (enc_w[0], own_w[0], got_w[0]), (enc_w[2], own_w[2], got_w[2])]
    loads += [(enc_w[1], own_w[1], got_w[1]), (dec_w[0], got_w[0], own_w[0]), (dec_w[1], got_w[1], own_w[1])]
    loads += [(dec_w[2], got_w[2].at[0 : taps_of[1]], own_w[2].at[0 : taps_of[1]]), (cot, got, rows.at[1])]

    def load(at):
        target, first, second = loads[at]
        pl.when(leading)(pltpu.make_async_copy(first, target, sem.at[at]).start)
        pl.when(jnp.logical_not(leading))(pltpu.make_async_copy(second, target, sem.at[at]).start)

    for at in range(4):
        load(at)

    def ready(at):
        pltpu.make_async_copy(loads[at][1], loads[at][0], sem.at[at]).wait()

    fill_columns(small[0], cols)
    hout_ones = dec_kept[9]
    dec_kept[9] = hout_ones.at[0:inner]
    hout_ones[inner:, :] = jnp.ones((16, tokens), BF)
    ready(0)

    def enc_ready(which):
        for at in ((1,), (2, 3))[which]:
            ready(at)
        if which:
            for at in range(4, 8):
                load(at)

    turned = (w_out_t, conv_t)
    forward_block(taps_of[0], begins, dilation[0], x, y_enc, enc_w, turned, cols, enc_kept, hmid, prod, enc_ready)
    saves = [pltpu.make_async_copy(a, b, sem.at[8 + i]) for i, (a, b) in enumerate(zip(enc_kept, kept_out))]
    start_all(saves)

    fill_columns(small[1], cols)
    for at in range(4, 8):
        ready(at)
    for k in range(taps_of[1]):
        conv_w[:, inner * k : inner * (k + 1)] = dec_w[2][k]
    y_dec = x
    forward_block(
        taps_of[1], begins, dilation[1], y_enc, y_dec, dec_w, turned, cols, dec_kept, hmid, prod, lambda which: None
    )
    pl.when(leading)(pltpu.make_async_copy(y_enc, outs.at[0], sem.at[18]).start)
    pl.when(leading)(pltpu.make_async_copy(y_dec, send_y, sem.at[19]).start)
    pl.when(jnp.logical_not(leading))(pltpu.make_async_copy(y_dec, outs.at[1], sem.at[18]).start)
    pl.when(jnp.logical_not(leading))(pltpu.make_async_copy(y_enc, send_y, sem.at[19]).start)

    n1, s1, r, n2, s2, n3, s3, hin, shifted, hout = dec_kept
    rows_out = RowsOut(buf, keep_buf, send_buf, section, index, groups, row_sems)
    w_in_at, end = layout(taps_of[1], width, inner)[2:4]

    bias = []

    def third_beside():
        bias.append(put_w_out(buf, hout_ones, cot))

    def first_beside():
        put_slabs(buf, w_in_at, nt(grad_projected[...], hin[...]))

    back_third(cot, dec_w[1], (n3, s3, r), prod, means, grad_mixed, ag3, ab3, third_beside)
    put_taps(buf, taps_of[1], width, shifted, grad_mixed)
    back_second(
        taps_of[1], begins, dilation[1], conv_w, (n2, s2, r), prod, means, grad_mixed, moved, grad_projected, ag2, ab2,
        lambda: None,
    )
    rows_out.start(0, w_in_at)
    back_first(cot, dec_w[0], (n1, s1, r), prod, means, grad_projected, gx, ag1, ab1, first_beside)
    rows_out.start(w_in_at, end)
    last = pltpu.make_async_copy(gx, grad_out, sem.at[20])
    last.start()
    g1, g2, g3 = gains_of(small[1], width, inner)
    first, second, third = gain_and_bias(g1, (ag1, ab1)), gain_and_bias(g2, (ag2, ab2)), gain_and_bias(g3, (ag3, ab3))
    put_vectors(vec_out, 0, vec, first + [second[0], third[0], second[1], third[1]] + bias)
    rows_out.wait()
    wait_all(saves + [last])
    pltpu.make_async_copy(y_enc, outs.at[0], sem.at[18]).wait()
    pltpu.make_async_copy(y_dec, send_y, sem.at[19]).wait()


def main_call(taps_of, groups, seq, rows, got, small_own, small_got, own_w, got_w):
    _, width, tokens = rows.shape
    inner = own_w[1].shape[0]
    half = padded_rows(layout(taps_of[1], width, inner)[3], groups) // 2
    wide, narrow = (width, tokens), (inner, tokens)
    weight_shapes = [(inner, width), (inner, width)]
    scratch = [(wide, BF)] * 2
    for taps in taps_of:
        scratch += [(dims, BF) for dims in weight_shapes + [(taps, inner, inner)]]
    scratch += [((SMALL_ROWS, width), F32)] * 2
    scratch += kept_shapes(taps_of[0], width, inner, tokens) + kept_shapes(taps_of[1], width, inner, tokens)[:-1]
    scratch += [((inner + 16, tokens), BF)]
    scratch += [(dims, F32) for dims in column_shapes(width, inner)]
    scratch += [
        (narrow, BF), (wide, F32), ((16, tokens), F32), (wide, BF), (wide, BF), ((width, inner), BF),
        ((inner, inner * taps_of[0]), BF), ((inner, inner * taps_of[1]), BF),
        (narrow, BF), (narrow, BF), ((inner * taps_of[1], tokens), BF), ((2 * half, LANES), BF),
    ]
    scratch += [((width, LANES), F32)] * 2 + [((inner, LANES), F32)] * 4 + [((VEC_ROWS, LANES), F32)]
    block = shape((half, LANES), BF)
    outs = [shape((2,) + wide, BF), shape(wide, BF), shape(wide, BF), block, block, shape((VEC_ROWS, LANES), BF)]
    outs += [shape(dims, dtype) for dims, dtype in kept_shapes(taps_of[0], width, inner, tokens)]
    flops = 2 * tokens * inner * (2 * width + taps_of[0] * inner + 3 * (2 * width + taps_of[1] * inner))
    return pl.pallas_call(
        functools.partial(main_kernel, taps_of, groups),
        in_specs=[SMEM, ANY, ANY, VMEM, VMEM] + [ANY] * 6,
        out_specs=[ANY] * 5 + [VMEM] + [ANY] * 10,
        out_shape=outs,
        scratch_shapes=[pltpu.VMEM(dims, dtype) for dims, dtype in scratch]
        + [pltpu.SemaphoreType.DMA((24,)), pltpu.SemaphoreType.DMA((8 * share_count(groups[0]),))],
        compiler_params=pltpu.CompilerParams(vmem_limit_bytes=VMEM_LIMIT),
        cost_estimate=pl.CostEstimate(flops=4 * flops, bytes_accessed=60 * 2**20, transcendentals=0),
        name="main_blocks",
    )(seq, rows, got, small_own, small_got, *own_w, *got_w)


def load_weight(leading, own, got, target, sem):
    pl.when(leading)(pltpu.make_async_copy(own, target, sem).start)
    pl.when(jnp.logical_not(leading))(pltpu.make_async_copy(got, target, sem).start)
    return pltpu.make_async_copy(own, target, sem)


def wait_all(copies):
    for copy in copies:
        copy.wait()


def encoder_kernel(
    taps, groups,
    seq, gy_in, small_own, small_got, n3_in, s3_in, r_in, shifted_in, hout_in, n2_in, s2_in, hin_in, own_out, got_out,
    own_conv, got_conv,
    grad_projected_out, vec_out, keep_buf, send_buf,
    gy, n3, s3, r, shifted, hout_ones, n2, s2, hin, w_out, conv, conv_w, prod, means, grad_mixed, moved, grad_projected,
    buf, ag3, ab3, ag2, ab2, sem, row_sems,
):
    section = lax.axis_index("section")
    leading = section == 0
    width, tokens = gy.shape
    inner = w_out.shape[0]
    w_in_at, end = layout(taps, width, inner)[2:4]
    hout = hout_ones.at[0:inner]
    pairs = (
        (gy_in, gy), (s3_in, s3), (n3_in, n3), (r_in, r), (hout_in, hout), (shifted_in, shifted), (n2_in, n2), (s2_in, s2),
        (hin_in, hin),
    )
    loads = [pltpu.make_async_copy(a, b, sem.at[2 + i]) for i, (a, b) in enumerate(pairs)]
    loads[0].start()
    weight = load_weight(leading, own_out, got_out, w_out, sem.at[0])
    start_all(loads[1:5])
    conv_weight = load_weight(leading, own_conv, got_conv, conv, sem.at[1])
    start_all(loads[5:])
    hout_ones[inner:, :] = jnp.ones((16, tokens), BF)
    small = pick_small(leading, small_own, small_got)
    dilation = jnp.max(small[7:8, 0:LANES]).astype(jnp.int32)

    def begins(unit):
        return seq[section, unit]

    def weights():
        conv_weight.wait()
        for k in range(taps):
            conv_w[:, inner * k : inner * (k + 1)] = conv[k]

    wait_all([weight, loads[0]])
    bias = []

    def third_beside():
        wait_all(loads[1:5])
        bias.append(put_w_out(buf, hout_ones, gy))

    back_third(gy, w_out, (n3, s3, r), prod, means, grad_mixed, ag3, ab3, third_beside)
    wait_all([loads[5]])
    put_taps(buf, taps, width, shifted, grad_mixed)
    back_second(
        taps, begins, dilation, conv_w, (n2, s2, r), prod, means, grad_mixed, moved, grad_projected, ag2, ab2,
        lambda: wait_all(loads[6:8]), weights,
    )
    out = pltpu.make_async_copy(grad_projected, grad_projected_out, sem.at[11])
    out.start()
    rows_out = RowsOut(buf, keep_buf, send_buf, section, lax.axis_index("dp"), groups, row_sems)
    rows_out.start(0, w_in_at)
    loads[8].wait()
    put_slabs(buf, w_in_at, nt(grad_projected[...], hin[...]))
    rows_out.start(w_in_at, end)
    _, g2, g3 = gains_of(small, width, inner)
    second, third = gain_and_bias(g2, (ag2, ab2)), gain_and_bias(g3, (ag3, ab3))
    put_rows(vec_out, [second[0], third[0], second[1], third[1]] + bias)
    out.wait()
    rows_out.wait()


def encoder_call(taps, groups, seq, gy, small_own, small_got, kept, own_out, got_out, own_conv, got_conv):
    width, tokens = gy.shape
    inner = own_out.shape[0]
    n1, s1, r, n2, s2, n3, s3, hin, shifted, hout = kept
    rows = layout(taps, width, inner)[3]
    half = padded_rows(rows, groups) // 2
    wide, narrow = (width, tokens), (inner, tokens)
    scratch = [
        (wide, BF), (narrow, BF), (narrow, BF), ((8, tokens), F32), ((inner * taps, tokens), BF),
        ((inner + 16, tokens), BF), (narrow, BF), (narrow, BF), (wide, BF), ((inner, width), BF),
        ((taps, inner, inner), BF), ((inner, inner * taps), BF), (narrow, F32), ((16, tokens), F32), (narrow, BF),
        ((inner * taps, tokens), BF), (narrow, BF), ((rows, LANES), BF),
    ]
    scratch += [((inner, LANES), F32)] * 4
    flops = 2 * tokens * inner * (3 * width + 2 * taps * inner)
    block = shape((half, LANES), BF)
    return pl.pallas_call(
        functools.partial(encoder_kernel, taps, groups),
        in_specs=[SMEM, ANY, VMEM, VMEM] + [ANY] * 12,
        out_specs=[ANY, VMEM, ANY, ANY],
        out_shape=[shape(narrow, BF), shape((SMALL_ROWS, width), F32), block, block],
        scratch_shapes=[pltpu.VMEM(dims, dtype) for dims, dtype in scratch]
        + [pltpu.SemaphoreType.DMA((12,)), pltpu.SemaphoreType.DMA((8 * share_count(groups[0]),))],
        compiler_params=pltpu.CompilerParams(vmem_limit_bytes=SMALL_LIMIT),
        cost_estimate=pl.CostEstimate(flops=4 * flops, bytes_accessed=20 * 2**20, transcendentals=0),
        name="encoder_back",
    )(
        seq, gy, small_own, small_got, n3, s3, r, shifted, hout, n2, s2, hin, own_out, got_out, own_conv, got_conv
    )


def first_kernel(
    block, gy_first, gy_second, grad_projected_in, small_own, small_got, vecs, n1_in, s1_in, r_in, own_in, got_in,
    *refs,
):
    outs_of, refs = refs[: 2 - block], refs[2 - block :]
    vec_out, gy, grad_projected, n1, s1, r, w_in_t, prod, means, gx, ag1, ab1, vec, sem = refs
    leading = lax.axis_index("section") == 0
    mine = leading if block == 0 else jnp.logical_not(leading)
    width, inner = gy.shape[0], grad_projected.shape[0]
    pairs = ((grad_projected_in, grad_projected), (s1_in, s1), (n1_in, n1), (r_in, r))
    loads = [pltpu.make_async_copy(a, b, sem.at[2 + i]) for i, (a, b) in enumerate(pairs)]
    loads[0].start()
    weight = load_weight(mine, own_in, got_in, w_in_t, sem.at[0])
    start_all(loads[1:])
    loads.append(load_weight(leading, gy_first, gy_second, gy, sem.at[1]))
    small = pick_small(mine, small_own, small_got)
    wait_all([loads[0], weight])

    def save(value, at_home, away, sem):
        pl.when(leading)(pltpu.make_async_copy(value, at_home, sem).start)
        pl.when(jnp.logical_not(leading))(pltpu.make_async_copy(value, away, sem).start)
        return pltpu.make_async_copy(value, away, sem)

    waits = []

    def ready():
        wait_all(loads[1:])
        if block == 0:
            outs, send = outs_of
            waits.append(save(gy, send, outs.at[1], sem.at[6]))

    back_first(gy, w_in_t, (n1, s1, r), prod, means, grad_projected, gx, ag1, ab1, ready)
    if block == 0:
        outs, send = outs_of
        waits.append(save(gx, outs.at[0], send, sem.at[7]))
    else:
        waits.append(pltpu.make_async_copy(gx, outs_of[0], sem.at[7]))
        waits[-1].start()
    sums = gain_and_bias(gains_of(small, width, inner)[0], (ag1, ab1))
    sums += [vecs[row : row + 1, 0:size] for row, size in enumerate((inner, inner, inner, inner, width))]
    put_vectors(vec_out, 0, vec, sums)
    wait_all(waits)


def first_call(block, gy_first, gy_second, grad_projected, vecs, kept, small_own, small_got, own_in, got_in):
    n1, s1, r = kept
    width, tokens = n1.shape
    inner = grad_projected.shape[0]
    wide, narrow = (width, tokens), (inner, tokens)
    scratch = [
        (wide, BF), (narrow, BF), (wide, BF), (wide, BF), ((8, tokens), F32), ((inner, width), BF), (wide, F32),
        ((16, tokens), F32), (wide, BF), ((width, LANES), F32), ((width, LANES), F32), ((VEC_ROWS, LANES), F32),
    ]
    outs = [shape((2,) + wide, BF), shape(wide, BF)] if block == 0 else [shape(wide, BF)]
    flops = 2 * tokens * inner * width
    return pl.pallas_call(
        functools.partial(first_kernel, block),
        in_specs=[ANY] * 3 + [VMEM] * 3 + [ANY] * 5,
        out_specs=[ANY] * len(outs) + [VMEM],
        out_shape=outs + [shape((VEC_ROWS, LANES), BF)],
        scratch_shapes=[pltpu.VMEM(dims, dtype) for dims, dtype in scratch] + [pltpu.SemaphoreType.DMA((8,))],
        compiler_params=pltpu.CompilerParams(vmem_limit_bytes=SMALL_LIMIT),
        cost_estimate=pl.CostEstimate(flops=8 * flops, bytes_accessed=20 * 2**20, transcendentals=0),
        name="first_%d" % block,
    )(gy_first, gy_second, grad_projected, small_own, small_got, vecs, n1, s1, r, own_in, got_in)


def load_weight(first, one, other, target, sem):
    pl.when(first)(pltpu.make_async_copy(one, target, sem).start)
    pl.when(jnp.logical_not(first))(pltpu.make_async_copy(other, target, sem).start)
    return pltpu.make_async_copy(one, target, sem)


def wait_all(copies):
    for copy in copies:
        copy.wait()


def unpack_kernel(taps_of, groups_of, *refs):
    refs = list(refs)

    def take(number):
        taken = refs[:number]
        del refs[:number]
        return taken

    own_of, got_of = [], []
    for _ in range(2):
        own_of.append(take(2))
        got_of.append(take(2))
    w_in_t_out, w_out_out, conv_out, gin, bin_, gmid, bmid, out_bias, w_in_t, w_out, conv, buf, extra, sem = refs
    inner, width = w_out.shape
    whole = inner // LANES
    tail = inner - whole * LANES
    slots = conv.shape[0]
    section = lax.axis_index("section")
    index = lax.axis_index("dp")

    def write(taps, groups, own, got):
        rows = own[0].shape[0] - VEC_ROWS
        count = share_count(groups[0])
        share = 2 * rows // count

        def body(position, _):
            for which, (pieces, side) in enumerate(((own, section), (got, 1 - section))):
                for at, ref in enumerate(pieces):
                    owner = owner_of(position + at * (count // 2), side, groups, index)
                    start = side * (2 * rows) + owner * share
                    pltpu.make_async_copy(
                        ref.at[pl.ds(pl.multiple_of(position * share, 16), share)],
                        buf.at[pl.ds(pl.multiple_of(start, 16), share)],
                        sem.at[2 * which + at],
                    ).start()
            return 0

        lax.fori_loop(0, count // 2, body, 0)
        pieces = list(own) + list(got)
        vectors = [
            pltpu.make_async_copy(ref.at[pl.ds(rows, VEC_ROWS)], extra.at[at], sem.at[4 + at])
            for at, ref in enumerate(pieces)
        ]
        start_all(vectors)
        for at, ref in enumerate(pieces):
            pltpu.make_async_copy(ref.at[pl.ds(0, rows)], buf.at[pl.ds(0, rows)], sem.at[at]).wait()
        wait_all(vectors)
        taps_at, tails_at, w_in_at, _, _ = layout(taps, width, inner)

        def wide(target, row):
            for at in range(0, width, LANES):
                q = at // LANES
                size = min(LANES, width - at)
                target[:, at : at + size] = buf[row + q * inner : row + (q + 1) * inner, 0:size].astype(F32)

        copies = []

        def leave(source, target):
            copies.append(pltpu.make_async_copy(source, target, sem.at[8 + len(copies)]))
            copies[-1].start()

        wide(w_out, 0)
        leave(w_out, w_out_out)
        tails = buf[tails_at : tails_at + inner, :].astype(F32)
        for k in range(slots):
            if k >= taps:
                conv[k] = jnp.zeros((inner, inner), F32)
            else:
                for q in range(whole):
                    at = taps_at + inner * (whole * k + q)
                    conv[k, :, LANES * q : LANES * (q + 1)] = buf[at : at + inner, :].astype(F32)
                conv[k, :, LANES * whole :] = tails[:, tail * k : tail * (k + 1)]
            leave(conv.at[k], conv_out.at[k])
        wide(w_in_t, w_in_at)
        leave(w_in_t, w_in_t_out)
        vec = sum(extra[at].astype(F32) for at in range(4))
        row = 0
        for target, member in ((gin, 0), (bin_, 0), (gmid, 0), (gmid, 1), (bmid, 0), (bmid, 1), (out_bias, 0)):
            for at in range(0, target.shape[1], LANES):
                size = min(LANES, target.shape[1] - at)
                target[member : member + 1, at : at + size] = vec[row : row + 1, 0:size]
                row += 1
        for copy in copies:
            copy.wait()

    pl.when(section == 0)(lambda: write(taps_of[0], groups_of[0], own_of[0], got_of[0]))
    pl.when(section != 0)(lambda: write(taps_of[1], groups_of[1], own_of[1], got_of[1]))


def unpack(taps_of, groups_of, enc, dec, width, inner):
    pieces = enc[0] + enc[1] + dec[0] + dec[1]
    rows = max(4 * part[0].shape[0] for part in (enc[0], dec[0]))
    return pl.pallas_call(
        functools.partial(unpack_kernel, taps_of, groups_of),
        in_specs=[ANY] * len(pieces),
        out_specs=[ANY] * 3 + [VMEM] * 5,
        out_shape=[
            shape((inner, width), F32), shape((inner, width), F32), shape((taps_of[0], inner, inner), F32),
            shape((1, width), F32), shape((1, width), F32), shape((2, inner), F32), shape((2, inner), F32),
            shape((1, width), F32),
        ],
        scratch_shapes=[
            pltpu.VMEM((inner, width), F32), pltpu.VMEM((inner, width), F32), pltpu.VMEM((taps_of[0], inner, inner), F32),
            pltpu.VMEM((rows, LANES), BF), pltpu.VMEM((4, VEC_ROWS, LANES), BF),
            pltpu.SemaphoreType.DMA((10 + taps_of[0],)),
        ],
        compiler_params=pltpu.CompilerParams(vmem_limit_bytes=SMALL_LIMIT),
        name="unpack",
    )(*pieces)


def swap_sections(value):
    return lax.ppermute(value, "section", [(0, 1), (1, 0)])


def swap_dp(value, masks):
    count = lax.axis_size("dp")
    pairs = [(s * count + i, s * count + (i ^ masks[s])) for s in range(2) for i in range(count)]
    return lax.ppermute(value, ("section", "dp"), pairs)


def rounded_sum(terms, rows):
    total = terms[0][rows].astype(F32)
    for term in terms[1:]:
        total = total + term[rows].astype(F32)
    return total.astype(BF)


def masks_of(bits, other):
    return [other << own[0] for own in bits]


def reduce_steps(keep, got, groups, receiver, vec=None):
    count = lax.axis_size("dp")
    steps = list(zip(*groups))
    terms = [keep, got]

    def loaded(part, riding):
        return part if vec is None or not riding else jnp.concatenate([part, vec], 0)

    for number, bits in enumerate(steps):
        size = terms[0].shape[0] >> len(bits[0])
        others = range(1, 2 ** len(bits[0]))
        parts = [rounded_sum(terms, slice(other * size, (other + 1) * size)) for other in others]
        parts = [loaded(part, number > 0) for part in parts]
        gate = yield parts
        came = after([swap_dp(part, masks_of(bits, other)) for part, other in zip(parts, others)], gate)
        terms = [term[:size] for term in terms] + [part[:size] for part in came]
        if vec is not None and number > 0:
            vec = rounded_sum([vec] + [part[size:] for part in came], slice(None))
    value = rounded_sum(terms, slice(None))
    rest = list(range(sum(len(bits) for bits in groups[0]), count.bit_length() - 1))
    for bits in zip(rest, rest[1:] + rest[:1]):
        size = value.shape[0]
        whole = loaded(value, True)
        gate = yield [whole]
        whole = rounded_sum([whole, after(swap_dp(whole, [1 << bit for bit in bits]), gate)], slice(None))
        value, vec = whole[:size], (None if vec is None else whole[size:])
    pieces = [value]
    for bits in reversed(steps[1:]):
        if len(pieces) > 1:
            value = jnp.concatenate(pieces, 0)
        gate = yield [value]
        came = [swap_dp(value, masks_of(bits, other)) for other in range(1, 2 ** len(bits[0]))]
        pieces = [value] + after(came, gate)
    if vec is not None:
        pieces = pieces + [vec]
    if len(pieces) > 1:
        value = jnp.concatenate(pieces, 0)
    gate = yield [value]
    sender = 1 - receiver
    masks = masks_of(steps[0], 1)
    ways = ((receiver, masks[receiver]), (sender, 0), (sender, masks[sender]))
    came = []
    for source, mask in ways:
        pairs = [(source * count + i, receiver * count + (i ^ mask)) for i in range(count)]
        came.append(lax.ppermute(value, ("section", "dp"), pairs))
    yield [value] + after(came, gate)


class Steps:
    def __init__(self, *args):
        self.steps = reduce_steps(*args)
        self.ready = next(self.steps)

    def step(self, gate=()):
        self.ready = self.steps.send(gate)
        return self.ready

    def finish(self):
        while len(self.ready) != 4:
            self.step()
        return self.ready[:2], self.ready[2:]


def after(values, earlier):
    return lax.optimization_barrier((values, earlier))[0] if earlier else values


def shards(
    section_inputs,
    seq_lengths,
    dilations,
    gains_in,
    biases_in,
    gains_mid,
    biases_mid,
    out_bias,
    w_in,
    w_out,
    conv_taps,
):
    section = lax.axis_index("section")
    count = lax.axis_size("dp")
    groups_of = (scatter_groups(count, False), scatter_groups(count, False))
    rows = jnp.swapaxes(section_inputs[0], 1, 2)
    width = rows.shape[1]
    inner = w_out.shape[1]
    taps_of = (conv_taps.shape[1], DEC_TAPS)

    own_w = (jnp.swapaxes(w_in[0], 0, 1), w_out[0], conv_taps[0])
    send_rows = pick_rows(rows)
    got_w = tuple(swap_sections(member) for member in own_w)
    got_rows = swap_sections(after(send_rows, got_w))
    small = pack_small(gains_in, biases_in, gains_mid[0], biases_mid[0], out_bias, dilations)
    got_small = swap_sections(small)

    outs, send_y, grad_dec, keep_dec, send_dec, vec, *kept = main_call(
        taps_of, groups_of[1], seq_lengths, rows, got_rows, small, got_small, own_w, got_w
    )
    dec = Steps(keep_dec, swap_sections(send_dec), groups_of[1], 1, vec)
    gradient = after(grad_dec, dec.ready)
    grad_projected, vec, keep_enc, send_enc = encoder_call(
        taps_of[0], groups_of[0], seq_lengths, gradient, small, got_small, kept, own_w[1], got_w[1], own_w[2], got_w[2]
    )
    got_y = swap_sections(send_y)
    enc_early = swap_sections(send_enc)
    grad_projected = after(grad_projected, dec.step())
    grads_x, send_gx, vec = first_call(
        0, grad_dec, grad_dec, grad_projected, vec, kept[0:3], small, got_small, own_w[0], got_w[0]
    )

    def joined(pair, got):
        pair = lax.dynamic_update_slice_in_dim(pair, got[None], 1 - section, 0)
        return jnp.swapaxes(pair, 1, 2)[None]

    enc = Steps(keep_enc, enc_early, groups_of[0], 0, vec)
    got_gx = swap_sections(send_gx)
    outputs = joined(outs, got_y)
    input_grads = joined(grads_x, got_gx)
    named = {"d": dec, "e": enc}
    last = ()
    for name in SEQ:
        if name in named:
            if len(named[name].ready) != 4:
                last = named[name].step(last)
        else:
            last = [*last, outputs if name == "y" else input_grads]
    enc = enc.finish()
    dec = dec.finish()
    grads = unpack(taps_of, groups_of, enc, dec, width, inner)
    return (
        outputs,
        input_grads,
        grads[3],
        grads[4],
        grads[5][None],
        grads[6][None],
        grads[7],
        jnp.swapaxes(grads[0], 0, 1)[None],
        grads[1][None],
        grads[2][None],
    )


def solution(mesh):
    in_specs = (
        P("section", None, "dp", None),
        P(None, "dp"),
        P("section"),
        P("section", None),
        P("section", None),
        P("section", None, None),
        P("section", None, None),
        P("section", None),
        P("section", None, None),
        P("section", None, None),
        P("section", None, None, None),
    )
    out_specs = (
        P("section", None, "dp", None),
        P("section", None, "dp", None),
        P("section", None),
        P("section", None),
        P("section", None, None),
        P("section", None, None),
        P("section", None),
        P("section", None, None),
        P("section", None, None),
        P("section", None, None, None),
    )
    return jax.shard_map(shards, mesh=mesh, in_specs=in_specs, out_specs=out_specs, check_vma=False)
```

profile of v0, /device:TPU:0, one launch (start us, length us, event | category | flops | bytes accessed | tf_op | source)
XLA Modules:
  0.0 165.2 jit_solution(2673771474405466448)
XLA Ops:
  0.6 0.5 collective-permute-start.2
  1.2 0.1 collective-permute-start
  1.2 0.4 collective-permute-start.1
  1.7 2.2 %pick_rows.1 = bf16[800,1024]{1,0:T(8,128)(2,1)} custom-call(bf16[2,800,1024]{2,1,0:T(8,128)(2,1)} %bitcast.27), custom_call_target="tpu_custom_call" | custom-call | bytes 8388608 | tf_op jit(solution)/shard_map/pick_rows/pallas_call | solution.py:438
  3.9 2.1 %collective-permute-done.refs_8_.got_in = bf16[400,800]{1,0:T(8,128)(2,1)S(1)} collective-permute-done((bf16[400,800]{1,0:T(8,128)(2,1)}, bf16[400,800]{1,0:T(8,128)(2,1)S(1)}, u32[]{:S(2)}, u32[]{:S(2)}) %collective-permute-start) | collective-permute-done | bytes 640032 | tf_op jit(solution)/shard_map/ppermute | solution.py:926
  6.0 1.0 collective-permute-done.1.refs_9_.got_out
  7.1 0.9 copy-done.17
  8.0 0.4 collective-permute-start.3
  9.0 1.4 pack_small.1.refs_3_.small_own
  10.4 0.1 collective-permute-start.4
  10.5 1.3 collective-permute-done.4.refs_4_.small_got
  11.8 0.6 copy-done.18
  12.4 1.2 copy-done.15
  13.5 36.8 %main_blocks.1 = (bf16[2,800,1024]{2,1,0:T(8,128)(2,1)}, bf16[800,1024]{1,0:T(8,128)(2,1)}, bf16[800,1024]{1,0:T(8,128)(2,1)}, bf16[4800,128]{1,0:T(8,128)(2,1)}...) custom-call(s32[2,8]{1,0:T(2,128)} %seq.1, ...), custom_call_target="tpu_custom_call" | custom-call | flops 39321600000 | bytes 62914560 | tf_op jit(solution)/shard_map/main_blocks/pallas_call | solution.py:617
  50.3 0.6 collective-permute-start.6
  50.9 2.8 %collective-permute-done.6 = bf16[4800,128]{1,0:T(8,128)(2,1)S(1)} collective-permute-done((bf16[4800,128]{1,0:T(8,128)(2,1)}, bf16[4800,128]{1,0:T(8,128)(2,1)S(1)}, u32[]{:S(2)}, u32[]{:S(2)}) %collective-permute-start.6) | collective-permute-done | bytes 1228832 | tf_op jit(solution)/shard_map/ppermute | solution.py:926
  53.6 1.7 %add_convert_fusion.1 = bf16[2400,128]{1,0:T(8,128)(2,1)S(1)} fusion(bf16[4800,128]{1,0:T(8,128)(2,1)S(1)} %collective-permute-done.6, bf16[4800,128]{1,0:T(8,128)(2,1)} %get-tuple-element.59), kind=kLoop, calls=%fused_computation.3 | loop fusion | flops 1228800 | bytes 1843200 | tf_op jit(solution)/shard_map/convert_element_type | solution.py:939
  55.3 2.8 %collective-permute-start.7 = (bf16[2400,128]{1,0:T(8,128)(2,1)S(1)}, bf16[2400,128]{1,0:T(8,128)(2,1)}, u32[]{:S(2)}, u32[]{:S(2)}) collective-permute-start(bf16[2400,128]{1,0:T(8,128)(2,1)S(1)} %add_convert_fusion.1), channel_id=1, source_target_pairs={{0,1},{1,0},{2,3},{3,2},{4,5},{5,4},{6,7},{7,6},{8,9},{9,8},{10,11... | collective-permute-start | bytes 1843208 | tf_op jit(solution)/shard_map/ppermute | solution.py:932
  58.1 14.2 %encoder_back.1 = (bf16[400,1024]{1,0:T(8,128)(2,1)}, f32[8,800]{1,0:T(8,128)}, bf16[6016,128]{1,0:T(8,128)(2,1)}, bf16[6016,128]{1,0:T(8,128)(2,1)}) custom-call(s32[2,8]{1,0:T(2,128)} %seq.1, bf16[800,1024]{1,0:T(8,128)(2,1)} %get-tuple-element.61.gy_in.gy_first.gy_second, f32[8,800]{1,0:T(8,128)} %pack_small.1.refs_3_.small_own, f32[8,800]{1,0:T(8,128)} %copy-done.18, ...), custom_call_target="tpu_custom_call" | custom-call | flops 20971520000 | bytes 20971520 | tf_op jit(solution)/shard_map/encoder_back/pallas_call | solution.py:721
  72.3 0.1 collective-permute-start.9
  72.4 1.2 add_convert_fusion.9
  73.6 1.5 collective-permute-start.11
  75.2 5.5 %collective-permute-done.11 = bf16[1248,128]{1,0:T(8,128)(2,1)S(1)} collective-permute-done((bf16[1248,128]{1,0:T(8,128)(2,1)S(1)}, bf16[1248,128]{1,0:T(8,128)(2,1)S(1)}, u32[]{:S(2)}, u32[]{:S(2)}) %collective-permute-start.11) | collective-permute-done | bytes 319520 | tf_op jit(solution)/shard_map/ppermute | solution.py:932
  80.7 1.3 add_convert_fusion.8
  82.0 0.7 pad_maximum_fusion.5
  82.8 1.6 collective-permute-start.12
  84.4 1.2 add_convert_fusion
  85.6 0.2 copy-done.3
  85.8 1.5 collective-permute-start.10
  87.3 8.7 %first_0.1 = (bf16[2,800,1024]{2,1,0:T(8,128)(2,1)}, bf16[800,1024]{1,0:T(8,128)(2,1)}, bf16[48,128]{1,0:T(8,128)(2,1)}) custom-call(bf16[800,1024]{1,0:T(8,128)(2,1)} %get-tuple-element.61.gy_in.gy_first.gy_second, bf16[800,1024]{1,0:T(8,128)(2,1)} %get-tuple-element.61.gy_in.gy_first.gy_second, bf16[400,1024]{1,0:T(8,128)(2,1)} %get-tuple-element.72.grad_projected_in, ...), custom_call_target="tpu_custom_call" | custom-call | flops 5242880000 | bytes 20971520 | tf_op jit(solution)/shard_map/first_0/pallas_call | solution.py:791
  96.0 1.1 add_convert_fusion.7
  97.0 0.9 collective-permute-done.10
  97.9 1.4 add_convert_fusion.5
  99.3 1.5 collective-permute-start.13
  100.9 1.3 bitcast_dynamic-update-slice_fusion.1
  102.1 0.7 copy-done.14
  102.9 2.6 %collective-permute-start.15 = (bf16[1248,128]{1,0:T(8,128)(2,1)S(1)}, bf16[1248,128]{1,0:T(8,128)(2,1)S(1)}, u32[]{:S(2)}, u32[]{:S(2)}) collective-permute-start(bf16[1248,128]{1,0:T(8,128)(2,1)S(1)} %add_convert_fusion.7), channel_id=1, source_target_pairs={{0,8},{1,9},{2,10},{3,11},{4,12},{5,13},{6,14},{7,15},{8,0},{9,1},... | collective-permute-start | bytes 958472 | tf_op jit(solution)/shard_map/ppermute | solution.py:932
  105.4 1.8 %collective-permute-done.13 = bf16[1552,128]{1,0:T(8,128)(2,1)S(1)} collective-permute-done((bf16[1552,128]{1,0:T(8,128)(2,1)S(1)}, bf16[1552,128]{1,0:T(8,128)(2,1)S(1)}, u32[]{:S(2)}, u32[]{:S(2)}) %collective-permute-start.13) | collective-permute-done | bytes 397344 | tf_op jit(solution)/shard_map/ppermute | solution.py:932
  107.2 1.4 add_convert_fusion.4
  108.7 0.5 collective-permute-start.14
  109.2 9.1 %collective-permute-done.15 = bf16[1248,128]{1,0:T(8,128)(2,1)S(1)} collective-permute-done((bf16[1248,128]{1,0:T(8,128)(2,1)S(1)}, bf16[1248,128]{1,0:T(8,128)(2,1)S(1)}, u32[]{:S(2)}, u32[]{:S(2)}) %collective-permute-start.15) | collective-permute-done | bytes 319520 | tf_op jit(solution)/shard_map/ppermute | solution.py:932
  118.3 0.1 add_convert_fusion.6
  118.4 0.5 collective-permute-start.17
  118.9 2.4 %collective-permute-done.14 = bf16[1552,128]{1,0:T(8,128)(2,1)S(1)} collective-permute-done((bf16[1552,128]{1,0:T(8,128)(2,1)S(1)}, bf16[1552,128]{1,0:T(8,128)(2,1)S(1)}, u32[]{:S(2)}, u32[]{:S(2)}) %collective-permute-start.14) | collective-permute-done | bytes 397344 | tf_op jit(solution)/shard_map/ppermute | solution.py:932
  121.2 0.1 add_convert_fusion.3
  121.3 2.0 %collective-permute-start.16 = (bf16[1552,128]{1,0:T(8,128)(2,1)S(1)}, bf16[1552,128]{1,0:T(8,128)(2,1)S(1)}, u32[]{:S(2)}, u32[]{:S(2)}) collective-permute-start(bf16[1552,128]{1,0:T(8,128)(2,1)S(1)} %add_convert_fusion.3), channel_id=1, source_target_pairs={{0,8},{1,9},{2,10},{3,11},{4,12},{5,13},{6,14},{7,15},{8,0},{9,1},... | collective-permute-start | bytes 1191944 | tf_op jit(solution)/shard_map/ppermute | solution.py:932
  123.3 0.2 bitcast_dynamic-update-slice_fusion
  123.6 1.7 %collective-permute-done.17 = bf16[1200,128]{1,0:T(8,128)(2,1)S(1)} collective-permute-done((bf16[1200,128]{1,0:T(8,128)(2,1)S(1)}, bf16[1200,128]{1,0:T(8,128)(2,1)S(1)}, u32[]{:S(2)}, u32[]{:S(2)}) %collective-permute-start.17) | collective-permute-done | bytes 307232 | tf_op jit(solution)/shard_map/ppermute | solution.py:932
  125.4 0.7 collective-permute-start.19
  126.1 1.3 collective-permute-start.20
  127.4 2.1 %collective-permute-start.21 = (bf16[2448,128]{1,0:T(8,128)(2,1)S(1)}, bf16[2448,128]{1,0:T(8,128)(2,1)S(1)}, u32[]{:S(2)}, u32[]{:S(2)}) collective-permute-start(bf16[2448,128]{1,0:T(8,128)(2,1)S(1)} %pad_maximum_fusion.1.refs_4_), channel_id=1, source_target_pairs={{0,17},{1,16},{2,19},{3,18},{4,21},{5,20},{6,23},{7,22},{8,25},{9,... | collective-permute-start | bytes 1880072 | tf_op jit(solution)/shard_map/ppermute | solution.py:990
  129.5 4.9 %collective-permute-done.16 = bf16[1552,128]{1,0:T(8,128)(2,1)S(1)} collective-permute-done((bf16[1552,128]{1,0:T(8,128)(2,1)S(1)}, bf16[1552,128]{1,0:T(8,128)(2,1)S(1)}, u32[]{:S(2)}, u32[]{:S(2)}) %collective-permute-start.16) | collective-permute-done | bytes 397344 | tf_op jit(solution)/shard_map/ppermute | solution.py:932
  134.4 0.1 add_convert_fusion.2
  134.5 0.1 collective-permute-start.18
  134.6 5.3 %collective-permute-done.21.refs_7_ = bf16[2448,128]{1,0:T(8,128)(2,1)S(1)} collective-permute-done((bf16[2448,128]{1,0:T(8,128)(2,1)S(1)}, bf16[2448,128]{1,0:T(8,128)(2,1)S(1)}, u32[]{:S(2)}, u32[]{:S(2)}) %collective-permute-start.21) | collective-permute-done | bytes 626720 | tf_op jit(solution)/shard_map/ppermute | solution.py:990
  140.0 0.8 copy-done.9
  140.8 1.5 collective-permute-done.18
  142.3 1.9 %collective-permute-start.22 = (bf16[3056,128]{1,0:T(8,128)(2,1)S(1)}, bf16[3056,128]{1,0:T(8,128)(2,1)S(1)}, u32[]{:S(2)}, u32[]{:S(2)}) collective-permute-start(bf16[3056,128]{1,0:T(8,128)(2,1)S(1)} %pad_maximum_fusion.refs_0_), channel_id=1, source_target_pairs={{0,1},{1,0},{2,3},{3,2},{4,5},{5,4},{6,7},{7,6},{8,9},{9,8},{10,11... | collective-permute-start | bytes 2347016 | tf_op jit(solution)/shard_map/ppermute | solution.py:990
  144.3 1.3 collective-permute-start.23
  145.6 1.3 collective-permute-start.24
  146.9 9.3 %collective-permute-done.22.refs_1_ = bf16[3056,128]{1,0:T(8,128)(2,1)S(1)} collective-permute-done((bf16[3056,128]{1,0:T(8,128)(2,1)S(1)}, bf16[3056,128]{1,0:T(8,128)(2,1)S(1)}, u32[]{:S(2)}, u32[]{:S(2)}) %collective-permute-start.22) | collective-permute-done | bytes 782368 | tf_op jit(solution)/shard_map/ppermute | solution.py:990
  156.2 0.9 copy-done.6
  157.1 2.3 %collective-permute-done.24.refs_3_ = bf16[3056,128]{1,0:T(8,128)(2,1)} collective-permute-done((bf16[3056,128]{1,0:T(8,128)(2,1)S(1)}, bf16[3056,128]{1,0:T(8,128)(2,1)}, u32[]{:S(2)}, u32[]{:S(2)}) %collective-permute-start.24) | collective-permute-done | bytes 782368 | tf_op jit(solution)/shard_map/ppermute | solution.py:990
  159.4 5.6 %unpack.1 = (f32[400,800]{1,0:T(8,128)}, f32[400,800]{1,0:T(8,128)}, f32[5,400,400]{2,1,0:T(8,128)}, f32[1,800]{1,0:T(1,128)}, f32[1,800]{1,0:T(1,128)}, /*index...) custom-call(bf16[3056,128]{1,0:T(8,128)(2,1)} %copy-done, bf16[3056,128]{1,0:T(8,128)(2,1)} %copy-done.5, ...), custom_call_target="tpu_custom_call" | custom-call | tf_op jit(solution)/shard_map/unpack/pallas_call | solution.py:906
  (54 shorter events, 0.3 us)
Async XLA Ops:
  0.6 7.3 %collective-permute-start.2 = (bf16[5,400,400]{2,1,0:T(8,128)(2,1)}, bf16[5,400,400]{2,1,0:T(8,128)(2,1)}, u32[]{:S(2)}, u32[]{:S(2)}) collective-permute-start(bf16[5,400,400]{2,1,0:T(8,128)(2,1)} %bitcast.34), channel_id=1, source_target_pairs={{0,16},{16,0},{1,17},{17,1},{2,18},{18,2},{3,19},{19,3},{4,20},{20... | collective-permute-start | bytes 4800008 | tf_op jit(solution)/shard_map/ppermute | solution.py:926
  1.2 4.9 %collective-permute-start = (bf16[400,800]{1,0:T(8,128)(2,1)}, bf16[400,800]{1,0:T(8,128)(2,1)S(1)}, u32[]{:S(2)}, u32[]{:S(2)}) collective-permute-start(bf16[400,800]{1,0:T(8,128)(2,1)} %bitcast.42), channel_id=1, source_target_pairs={{0,16},{16,0},{1,17},{17,1},{2,18},{18,2},{3,19},{19,3},{4,20},{20... | collective-permute-start | bytes 1920008 | tf_op jit(solution)/shard_map/ppermute | solution.py:926
  1.2 5.8 %collective-permute-start.1 = (bf16[400,800]{1,0:T(8,128)(2,1)}, bf16[400,800]{1,0:T(8,128)(2,1)S(1)}, u32[]{:S(2)}, u32[]{:S(2)}) collective-permute-start(bf16[400,800]{1,0:T(8,128)(2,1)} %bitcast.39), channel_id=1, source_target_pairs={{0,16},{16,0},{1,17},{17,1},{2,18},{18,2},{3,19},{19,3},{4,20},{20... | collective-permute-start | bytes 1920008 | tf_op jit(solution)/shard_map/ppermute | solution.py:926
  6.0 1.0 copy-start.16
  7.1 0.9 copy-start.17
  8.0 3.8 %collective-permute-start.3 = (bf16[800,1024]{1,0:T(8,128)(2,1)}, bf16[800,1024]{1,0:T(8,128)(2,1)S(1)}, u32[]{:S(2)}, u32[]{:S(2)}) collective-permute-start(bf16[800,1024]{1,0:T(8,128)(2,1)} %pick_rows.1), channel_id=1, source_target_pairs={{0,16},{16,0},{1,17},{17,1},{2,18},{18,2},{3,19},{19,3},{4,20},{20... | collective-permute-start | bytes 4915208 | tf_op jit(solution)/shard_map/ppermute | solution.py:926
  10.4 1.4 collective-permute-start.4
  11.8 0.6 copy-start.18
  12.4 1.2 copy-start.15
  50.3 3.3 %collective-permute-start.6 = (bf16[4800,128]{1,0:T(8,128)(2,1)}, bf16[4800,128]{1,0:T(8,128)(2,1)S(1)}, u32[]{:S(2)}, u32[]{:S(2)}) collective-permute-start(bf16[4800,128]{1,0:T(8,128)(2,1)} %get-tuple-element.60), channel_id=1, source_target_pairs={{0,16},{16,0},{1,17},{17,1},{2,18},{18,2},{3,19},{19,3},{4,20},{20... | collective-permute-start | bytes 3686408 | tf_op jit(solution)/shard_map/ppermute | solution.py:926
  53.6 18.8 %copy-start.4 = (bf16[4800,128]{1,0:T(8,128)(2,1)}, bf16[4800,128]{1,0:T(8,128)(2,1)S(1)}, u32[]{:S(2)}) copy-start(bf16[4800,128]{1,0:T(8,128)(2,1)S(1)} %collective-permute-done.6) | copy-start | bytes 3686404
  55.3 17.1 %collective-permute-start.7 = (bf16[2400,128]{1,0:T(8,128)(2,1)S(1)}, bf16[2400,128]{1,0:T(8,128)(2,1)}, u32[]{:S(2)}, u32[]{:S(2)}) collective-permute-start(bf16[2400,128]{1,0:T(8,128)(2,1)S(1)} %add_convert_fusion.1), channel_id=1, source_target_pairs={{0,1},{1,0},{2,3},{3,2},{4,5},{5,4},{6,7},{7,6},{8,9},{9,8},{10,11... | collective-permute-start | bytes 1843208 | tf_op jit(solution)/shard_map/ppermute | solution.py:932
  58.1 15.5 %copy-start.11 = (bf16[48,128]{1,0:T(8,128)(2,1)S(1)}, bf16[48,128]{1,0:T(8,128)(2,1)}, u32[]{:S(2)}) copy-start(bf16[48,128]{1,0:T(8,128)(2,1)} %get-tuple-element.71) | copy-start | bytes 36868
  72.3 12.1 %collective-permute-start.9 = (bf16[6016,128]{1,0:T(8,128)(2,1)}, bf16[6016,128]{1,0:T(8,128)(2,1)S(1)}, u32[]{:S(2)}, u32[]{:S(2)}) collective-permute-start(bf16[6016,128]{1,0:T(8,128)(2,1)} %get-tuple-element.79), channel_id=1, source_target_pairs={{0,16},{16,0},{1,17},{17,1},{2,18},{18,2},{3,19},{19,3},{4,20},{20... | collective-permute-start | bytes 4620296 | tf_op jit(solution)/shard_map/ppermute | solution.py:926
  73.6 10.8 %copy-start.2 = (bf16[6016,128]{1,0:T(8,128)(2,1)S(1)}, bf16[6016,128]{1,0:T(8,128)(2,1)}, u32[]{:S(2)}) copy-start(bf16[6016,128]{1,0:T(8,128)(2,1)} %get-tuple-element.78) | copy-start | bytes 4620292
  73.6 7.1 %collective-permute-start.11 = (bf16[1248,128]{1,0:T(8,128)(2,1)S(1)}, bf16[1248,128]{1,0:T(8,128)(2,1)S(1)}, u32[]{:S(2)}, u32[]{:S(2)}) collective-permute-start(bf16[1248,128]{1,0:T(8,128)(2,1)S(1)} %pad_maximum_fusion.4), channel_id=1, source_target_pairs={{0,2},{1,3},{2,0},{3,1},{4,6},{5,7},{6,4},{7,5},{8,10},{9,11},{10,... | collective-permute-start | bytes 958472 | tf_op jit(solution)/shard_map/ppermute | solution.py:932
  75.2 25.7 %collective-permute-start.5 = (bf16[800,1024]{1,0:T(8,128)(2,1)}, bf16[800,1024]{1,0:T(8,128)(2,1)S(1)}, u32[]{:S(2)}, u32[]{:S(2)}) collective-permute-start(bf16[800,1024]{1,0:T(8,128)(2,1)} %get-tuple-element.57), channel_id=1, source_target_pairs={{0,16},{16,0},{1,17},{17,1},{2,18},{18,2},{3,19},{19,3},{4,20},{20... | collective-permute-start | bytes 4915208 | tf_op jit(solution)/shard_map/ppermute | solution.py:926
  82.8 13.2 %collective-permute-start.12 = (bf16[1248,128]{1,0:T(8,128)(2,1)}, bf16[1248,128]{1,0:T(8,128)(2,1)}, u32[]{:S(2)}, u32[]{:S(2)}) collective-permute-start(bf16[1248,128]{1,0:T(8,128)(2,1)} %pad_maximum_fusion.5), channel_id=1, source_target_pairs={{0,4},{1,5},{2,6},{3,7},{4,0},{5,1},{6,2},{7,3},{8,12},{9,13},{10,... | collective-permute-start | bytes 958472 | tf_op jit(solution)/shard_map/ppermute | solution.py:932
  84.4 1.4 copy-start.3
  85.8 12.1 %collective-permute-start.10 = (bf16[3008,128]{1,0:T(8,128)(2,1)}, bf16[3008,128]{1,0:T(8,128)(2,1)}, u32[]{:S(2)}, u32[]{:S(2)}) collective-permute-start(bf16[3008,128]{1,0:T(8,128)(2,1)} %add_convert_fusion), channel_id=1, source_target_pairs={{0,1},{1,0},{2,3},{3,2},{4,5},{5,4},{6,7},{7,6},{8,9},{9,8},{10,11... | collective-permute-start | bytes 2310152 | tf_op jit(solution)/shard_map/ppermute | solution.py:932
  96.0 3.3 %copy-start.10 = (bf16[48,128]{1,0:T(8,128)(2,1)S(1)}, bf16[48,128]{1,0:T(8,128)(2,1)}, u32[]{:S(2)}) copy-start(bf16[48,128]{1,0:T(8,128)(2,1)} %get-tuple-element.82) | copy-start | bytes 36868
  99.3 7.9 %collective-permute-start.13 = (bf16[1552,128]{1,0:T(8,128)(2,1)S(1)}, bf16[1552,128]{1,0:T(8,128)(2,1)S(1)}, u32[]{:S(2)}, u32[]{:S(2)}) collective-permute-start(bf16[1552,128]{1,0:T(8,128)(2,1)S(1)} %pad_maximum_fusion.2), channel_id=1, source_target_pairs={{0,2},{1,3},{2,0},{3,1},{4,6},{5,7},{6,4},{7,5},{8,10},{9,11},{10,... | collective-permute-start | bytes 1191944 | tf_op jit(solution)/shard_map/ppermute | solution.py:932
  100.9 2.0 %copy-start.14 = (bf16[800,1024]{1,0:T(8,128)(2,1)S(1)}, bf16[800,1024]{1,0:T(8,128)(2,1)}, u32[]{:S(2)}) copy-start(bf16[800,1024]{1,0:T(8,128)(2,1)} %get-tuple-element.77) | copy-start | bytes 4915204
  102.9 20.4 %collective-permute-start.8 = (bf16[800,1024]{1,0:T(8,128)(2,1)S(1)}, bf16[800,1024]{1,0:T(8,128)(2,1)S(1)}, u32[]{:S(2)}, u32[]{:S(2)}) collective-permute-start(bf16[800,1024]{1,0:T(8,128)(2,1)S(1)} %copy-done.14), channel_id=1, source_target_pairs={{0,16},{16,0},{1,17},{17,1},{2,18},{18,2},{3,19},{19,3},{4,20},{20... | collective-permute-start | bytes 4915208 | tf_op jit(solution)/shard_map/ppermute | solution.py:926
  102.9 15.4 %collective-permute-start.15 = (bf16[1248,128]{1,0:T(8,128)(2,1)S(1)}, bf16[1248,128]{1,0:T(8,128)(2,1)S(1)}, u32[]{:S(2)}, u32[]{:S(2)}) collective-permute-start(bf16[1248,128]{1,0:T(8,128)(2,1)S(1)} %add_convert_fusion.7), channel_id=1, source_target_pairs={{0,8},{1,9},{2,10},{3,11},{4,12},{5,13},{6,14},{7,15},{8,0},{9,1},... | collective-permute-start | bytes 958472 | tf_op jit(solution)/shard_map/ppermute | solution.py:932
  108.7 14.7 %copy-start.12 = (bf16[2,800,1024]{2,1,0:T(8,128)(2,1)S(1)}, bf16[2,800,1024]{2,1,0:T(8,128)(2,1)}, u32[]{:S(2)}) copy-start(bf16[2,800,1024]{2,1,0:T(8,128)(2,1)} %get-tuple-element.76) | copy-start | bytes 9830404
  108.7 12.5 %collective-permute-start.14 = (bf16[1552,128]{1,0:T(8,128)(2,1)S(1)}, bf16[1552,128]{1,0:T(8,128)(2,1)S(1)}, u32[]{:S(2)}, u32[]{:S(2)}) collective-permute-start(bf16[1552,128]{1,0:T(8,128)(2,1)S(1)} %pad_maximum_fusion.3), channel_id=1, source_target_pairs={{0,4},{1,5},{2,6},{3,7},{4,0},{5,1},{6,2},{7,3},{8,12},{9,13},{10,... | collective-permute-start | bytes 1191944 | tf_op jit(solution)/shard_map/ppermute | solution.py:932
  118.4 6.9 %collective-permute-start.17 = (bf16[1200,128]{1,0:T(8,128)(2,1)S(1)}, bf16[1200,128]{1,0:T(8,128)(2,1)S(1)}, u32[]{:S(2)}, u32[]{:S(2)}) collective-permute-start(bf16[1200,128]{1,0:T(8,128)(2,1)S(1)} %slice.124), channel_id=1, source_target_pairs={{0,2},{1,3},{2,0},{3,1},{4,6},{5,7},{6,4},{7,5},{8,10},{9,11},{10,... | collective-permute-start | bytes 921608 | tf_op jit(solution)/shard_map/ppermute | solution.py:932
  121.3 13.0 %collective-permute-start.16 = (bf16[1552,128]{1,0:T(8,128)(2,1)S(1)}, bf16[1552,128]{1,0:T(8,128)(2,1)S(1)}, u32[]{:S(2)}, u32[]{:S(2)}) collective-permute-start(bf16[1552,128]{1,0:T(8,128)(2,1)S(1)} %add_convert_fusion.3), channel_id=1, source_target_pairs={{0,8},{1,9},{2,10},{3,11},{4,12},{5,13},{6,14},{7,15},{8,0},{9,1},... | collective-permute-start | bytes 1191944 | tf_op jit(solution)/shard_map/ppermute | solution.py:932
  123.5 32.7 %copy-start.13 = (bf16[2,800,1024]{2,1,0:T(8,128)(2,1)}, bf16[2,800,1024]{2,1,0:T(8,128)(2,1)S(1)}, u32[]{:S(2)}) copy-start(bf16[2,800,1024]{2,1,0:T(8,128)(2,1)S(1)} %bitcast_dynamic-update-slice_fusion) | copy-start | bytes 9830404
  125.3 17.0 %copy-start.1 = (bf16[2448,128]{1,0:T(8,128)(2,1)}, bf16[2448,128]{1,0:T(8,128)(2,1)S(1)}, u32[]{:S(2)}) copy-start(bf16[2448,128]{1,0:T(8,128)(2,1)S(1)} %pad_maximum_fusion.1.refs_4_) | copy-start | bytes 1880068
  125.4 9.3 %collective-permute-start.19 = (bf16[2448,128]{1,0:T(8,128)(2,1)S(1)}, bf16[2448,128]{1,0:T(8,128)(2,1)S(1)}, u32[]{:S(2)}, u32[]{:S(2)}) collective-permute-start(bf16[2448,128]{1,0:T(8,128)(2,1)S(1)} %pad_maximum_fusion.1.refs_4_), channel_id=1, source_target_pairs={{16,18},{17,19},{18,16},{19,17},{20,22},{21,23},{22,20},{23,21},{2... | collective-permute-start | bytes 1880072 | tf_op jit(solution)/shard_map/ppermute | solution.py:990
  126.1 8.6 %collective-permute-start.20 = (bf16[2448,128]{1,0:T(8,128)(2,1)S(1)}, bf16[2448,128]{1,0:T(8,128)(2,1)S(1)}, u32[]{:S(2)}, u32[]{:S(2)}) collective-permute-start(bf16[2448,128]{1,0:T(8,128)(2,1)S(1)} %pad_maximum_fusion.1.refs_4_), channel_id=1, source_target_pairs={{0,16},{1,17},{2,18},{3,19},{4,20},{5,21},{6,22},{7,23},{8,24},{9,... | collective-permute-start | bytes 1880072 | tf_op jit(solution)/shard_map/ppermute | solution.py:990
  127.4 12.6 %collective-permute-start.21 = (bf16[2448,128]{1,0:T(8,128)(2,1)S(1)}, bf16[2448,128]{1,0:T(8,128)(2,1)S(1)}, u32[]{:S(2)}, u32[]{:S(2)}) collective-permute-start(bf16[2448,128]{1,0:T(8,128)(2,1)S(1)} %pad_maximum_fusion.1.refs_4_), channel_id=1, source_target_pairs={{0,17},{1,16},{2,19},{3,18},{4,21},{5,20},{6,23},{7,22},{8,25},{9,... | collective-permute-start | bytes 1880072 | tf_op jit(solution)/shard_map/ppermute | solution.py:990
  134.5 7.8 %collective-permute-start.18 = (bf16[1504,128]{1,0:T(8,128)(2,1)S(1)}, bf16[1504,128]{1,0:T(8,128)(2,1)S(1)}, u32[]{:S(2)}, u32[]{:S(2)}) collective-permute-start(bf16[1504,128]{1,0:T(8,128)(2,1)S(1)} %slice.126), channel_id=1, source_target_pairs={{0,2},{1,3},{2,0},{3,1},{4,6},{5,7},{6,4},{7,5},{8,10},{9,11},{10,... | collective-permute-start | bytes 1155080 | tf_op jit(solution)/shard_map/ppermute | solution.py:932
  134.6 5.4 %copy-start.7 = (bf16[2448,128]{1,0:T(8,128)(2,1)}, bf16[2448,128]{1,0:T(8,128)(2,1)S(1)}, u32[]{:S(2)}) copy-start(bf16[2448,128]{1,0:T(8,128)(2,1)S(1)} %collective-permute-done.19.refs_5_) | copy-start | bytes 1880068
  134.6 5.3 %copy-start.8 = (bf16[2448,128]{1,0:T(8,128)(2,1)}, bf16[2448,128]{1,0:T(8,128)(2,1)S(1)}, u32[]{:S(2)}) copy-start(bf16[2448,128]{1,0:T(8,128)(2,1)S(1)} %collective-permute-done.20.refs_6_) | copy-start | bytes 1880068
  140.0 0.8 copy-start.9
  142.3 17.1 %copy-start = (bf16[3056,128]{1,0:T(8,128)(2,1)}, bf16[3056,128]{1,0:T(8,128)(2,1)S(1)}, u32[]{:S(2)}) copy-start(bf16[3056,128]{1,0:T(8,128)(2,1)S(1)} %pad_maximum_fusion.refs_0_) | copy-start | bytes 2347012
  142.3 13.8 %collective-permute-start.22 = (bf16[3056,128]{1,0:T(8,128)(2,1)S(1)}, bf16[3056,128]{1,0:T(8,128)(2,1)S(1)}, u32[]{:S(2)}, u32[]{:S(2)}) collective-permute-start(bf16[3056,128]{1,0:T(8,128)(2,1)S(1)} %pad_maximum_fusion.refs_0_), channel_id=1, source_target_pairs={{0,1},{1,0},{2,3},{3,2},{4,5},{5,4},{6,7},{7,6},{8,9},{9,8},{10,11... | collective-permute-start | bytes 2347016 | tf_op jit(solution)/shard_map/ppermute | solution.py:990
  144.3 11.9 %collective-permute-start.23 = (bf16[3056,128]{1,0:T(8,128)(2,1)S(1)}, bf16[3056,128]{1,0:T(8,128)(2,1)S(1)}, u32[]{:S(2)}, u32[]{:S(2)}) collective-permute-start(bf16[3056,128]{1,0:T(8,128)(2,1)S(1)} %pad_maximum_fusion.refs_0_), channel_id=1, source_target_pairs={{16,0},{17,1},{18,2},{19,3},{20,4},{21,5},{22,6},{23,7},{24,8},{25... | collective-permute-start | bytes 2347016 | tf_op jit(solution)/shard_map/ppermute | solution.py:990
  145.6 13.8 %collective-permute-start.24 = (bf16[3056,128]{1,0:T(8,128)(2,1)S(1)}, bf16[3056,128]{1,0:T(8,128)(2,1)}, u32[]{:S(2)}, u32[]{:S(2)}) collective-permute-start(bf16[3056,128]{1,0:T(8,128)(2,1)S(1)} %pad_maximum_fusion.refs_0_), channel_id=1, source_target_pairs={{16,2},{17,3},{18,0},{19,1},{20,6},{21,7},{22,4},{23,5},{24,10},{2... | collective-permute-start | bytes 2347016 | tf_op jit(solution)/shard_map/ppermute | solution.py:990
  156.2 3.2 %copy-start.5 = (bf16[3056,128]{1,0:T(8,128)(2,1)}, bf16[3056,128]{1,0:T(8,128)(2,1)S(1)}, u32[]{:S(2)}) copy-start(bf16[3056,128]{1,0:T(8,128)(2,1)S(1)} %collective-permute-done.22.refs_1_) | copy-start | bytes 2347012
  156.2 0.9 copy-start.6
where the time goes:
time: 166 us; the launch traced here: 165 us
  Pallas kernels  68.8 us (41%)
  waiting for transfers between devices  51.8 us (31%)
  starting transfers between devices  25.4 us (15%)
  other arithmetic  10.5 us (6%)
  local copies, waits for them, and re-layouts  6.89 us (4%)
  between operations  1.84 us (1%)
    pallas_call x1, Pallas kernels, main_call(): pl.pallas_call(functools.partial(main_kernel, taps_of, groups), in_specs=...  36.8 us
    ppermute x10, waiting for transfers between devices, swap_dp(): return lax.ppermute(value, ('section', 'dp'), pairs)  27.7 us
    ppermute x6, waiting for transfers between devices, reduce_steps(): came.append(lax.ppermute(value, ('section', 'dp'), pairs))  16.9 us
    ppermute x10, starting transfers between devices, swap_dp(): return lax.ppermute(value, ('section', 'dp'), pairs)  14.5 us
    pallas_call x1, Pallas kernels, encoder_call(): pl.pallas_call(functools.partial(encoder_kernel, taps, groups), in_specs=...  14.2 us
    convert_element_type x12, other arithmetic, rounded_sum(): return total.astype(BF)  9.58 us
    pallas_call x1, Pallas kernels, first_call(): pl.pallas_call(functools.partial(first_kernel, block), in_specs=[ANY] * 3...  8.68 us
    ppermute x6, starting transfers between devices, reduce_steps(): came.append(lax.ppermute(value, ('section', 'dp'), pairs))  8.64 us
  transfers between devices with their start and end apart: 25, of which 15 were waited for; matrix products, arithmetic and copies ran while one was open for 6% of the time, Pallas kernels for 16%

commit v1 on v0

--- a/solution.py
+++ b/solution.py
@@ -184,12 +184,24 @@
 
 
 def layout(taps, width, inner):
-    wide = pl.cdiv(width, LANES) * inner
+    wide = width // LANES * inner
     taps_at = wide
-    tails_at = taps_at + taps * (inner // LANES) * inner
-    w_in_at = tails_at + inner
-    vec_at = w_in_at + wide
-    return taps_at, tails_at, w_in_at, vec_at, vec_at + VEC_ROWS
+    w_in_at = taps_at + taps * (inner // LANES) * inner
+    tails_at = w_in_at + wide
+    (_, _), (last, _) = tail_places(taps, width, inner)
+    return taps_at, w_in_at, tails_at, tails_at + (last + 1) * inner
+
+
+def tail_places(taps, width, inner):
+    size = width % LANES
+    places = []
+    group, lane = 0, taps * (inner % LANES)
+    for _ in range(2):
+        if lane + size > LANES:
+            group, lane = group + 1, 0
+        places.append((group, lane))
+        lane += size
+    return places
 
 
 def scatter_groups(count, full):
@@ -207,18 +219,20 @@
     return pl.cdiv(rows, unit) * unit
 
 
-def put_slabs(buf, row, matrix):
+def put_wide(buf, row, matrix, tails_at, place):
     rows, cols = matrix.shape
-    for q in range(pl.cdiv(cols, LANES)):
-        part = matrix[:, LANES * q : min(cols, LANES * (q + 1))]
-        if part.shape[1] < LANES:
-            part = jnp.concatenate([part, jnp.zeros((rows, LANES - part.shape[1]), F32)], 1)
-        buf[row + q * rows : row + (q + 1) * rows, :] = part.astype(BF)
+    whole = cols // LANES
+    for q in range(whole):
+        buf[row + q * rows : row + (q + 1) * rows, :] = matrix[:, LANES * q : LANES * (q + 1)].astype(BF)
+    if cols > whole * LANES:
+        group, lane = place
+        at = tails_at + group * rows
+        buf[at : at + rows, lane : lane + cols - whole * LANES] = matrix[:, LANES * whole :].astype(BF)
 
 
 def put_taps(buf, taps, width, shifted, grad_mixed):
     inner = grad_mixed.shape[0]
-    taps_at, tails_at, _, _, _ = layout(taps, width, inner)
+    taps_at, _, tails_at, _ = layout(taps, width, inner)
     whole = inner // LANES
     tail = inner - whole * LANES
     for k in range(taps):
@@ -227,7 +241,6 @@
             at = taps_at + inner * (whole * k + q)
             buf[at : at + inner, :] = grad[:, LANES * q : LANES * (q + 1)].astype(BF)
         buf[tails_at : tails_at + inner, tail * k : tail * (k + 1)] = grad[:, LANES * whole :].astype(BF)
-    buf[tails_at : tails_at + inner, tail * taps :] = jnp.zeros((inner, LANES - tail * taps), BF)
 
 
 def row_sums(acc):
@@ -387,11 +400,19 @@
     norm_backward(prod, s1, n1, r, 0, gain_sums, bias_sums, means, emit, LOOPS[2])
 
 
-def put_w_out(buf, hout_ones, gy):
+def put_w_out(buf, taps, hout_ones, gy):
     grad = nt(hout_ones[...], gy[...])
-    inner = hout_ones.shape[0] - 16
-    put_slabs(buf, 0, grad[0:inner])
+    inner, width = hout_ones.shape[0] - 16, gy.shape[0]
+    _, _, tails_at, end = layout(taps, width, inner)
+    buf[tails_at:end, :] = jnp.zeros((end - tails_at, LANES), BF)
+    put_wide(buf, 0, grad[0:inner], tails_at, tail_places(taps, width, inner)[0])
     return grad[inner : inner + 1]
+
+
+def put_w_in(buf, taps, grad_projected, hin):
+    inner, width = grad_projected.shape[0], hin.shape[0]
+    _, w_in_at, tails_at, _ = layout(taps, width, inner)
+    put_wide(buf, w_in_at, nt(grad_projected[...], hin[...]), tails_at, tail_places(taps, width, inner)[1])
 
 
 def gain_and_bias(gain, sums):
@@ -561,15 +582,15 @@
 
     n1, s1, r, n2, s2, n3, s3, hin, shifted, hout = dec_kept
     rows_out = RowsOut(buf, keep_buf, send_buf, section, index, groups, row_sems)
-    w_in_at, end = layout(taps_of[1], width, inner)[2:4]
+    w_in_at, _, end = layout(taps_of[1], width, inner)[1:]
 
     bias = []
 
     def third_beside():
-        bias.append(put_w_out(buf, hout_ones, cot))
+        bias.append(put_w_out(buf, taps_of[1], hout_ones, cot))
 
     def first_beside():
-        put_slabs(buf, w_in_at, nt(grad_projected[...], hin[...]))
+        put_w_in(buf, taps_of[1], grad_projected, hin)
 
     back_third(cot, dec_w[1], (n3, s3, r), prod, means, grad_mixed, ag3, ab3, third_beside)
     put_taps(buf, taps_of[1], width, shifted, grad_mixed)
@@ -650,7 +671,7 @@
     leading = section == 0
     width, tokens = gy.shape
     inner = w_out.shape[0]
-    w_in_at, end = layout(taps, width, inner)[2:4]
+    w_in_at, _, end = layout(taps, width, inner)[1:]
     hout = hout_ones.at[0:inner]
     pairs = (
         (gy_in, gy), (s3_in, s3), (n3_in, n3), (r_in, r), (hout_in, hout), (shifted_in, shifted), (n2_in, n2), (s2_in, s2),
@@ -679,7 +700,7 @@
 
     def third_beside():
         wait_all(loads[1:5])
-        bias.append(put_w_out(buf, hout_ones, gy))
+        bias.append(put_w_out(buf, taps, hout_ones, gy))
 
     back_third(gy, w_out, (n3, s3, r), prod, means, grad_mixed, ag3, ab3, third_beside)
     wait_all([loads[5]])
@@ -693,7 +714,7 @@
     rows_out = RowsOut(buf, keep_buf, send_buf, section, lax.axis_index("dp"), groups, row_sems)
     rows_out.start(0, w_in_at)
     loads[8].wait()
-    put_slabs(buf, w_in_at, nt(grad_projected[...], hin[...]))
+    put_w_in(buf, taps, grad_projected, hin)
     rows_out.start(w_in_at, end)
     _, g2, g3 = gains_of(small, width, inner)
     second, third = gain_and_bias(g2, (ag2, ab2)), gain_and_bias(g3, (ag3, ab3))
@@ -858,13 +879,19 @@
         for at, ref in enumerate(pieces):
             pltpu.make_async_copy(ref.at[pl.ds(0, rows)], buf.at[pl.ds(0, rows)], sem.at[at]).wait()
         wait_all(vectors)
-        taps_at, tails_at, w_in_at, _, _ = layout(taps, width, inner)
-
-        def wide(target, row):
-            for at in range(0, width, LANES):
-                q = at // LANES
-                size = min(LANES, width - at)
-                target[:, at : at + size] = buf[row + q * inner : row + (q + 1) * inner, 0:size].astype(F32)
+        taps_at, w_in_at, tails_at, _ = layout(taps, width, inner)
+        places = tail_places(taps, width, inner)
+
+        def wide(target, row, place):
+            groups = width // LANES
+            for q in range(groups):
+                at = row + q * inner
+                target[:, LANES * q : LANES * (q + 1)] = buf[at : at + inner, :].astype(F32)
+            if width > groups * LANES:
+                group, lane = place
+                at = tails_at + group * inner
+                rest = buf[at : at + inner, :].astype(F32)
+                target[:, LANES * groups :] = rest[:, lane : lane + width - groups * LANES]
 
         copies = []
 
@@ -872,7 +899,7 @@
             copies.append(pltpu.make_async_copy(source, target, sem.at[8 + len(copies)]))
             copies[-1].start()
 
-        wide(w_out, 0)
+        wide(w_out, 0, places[0])
         leave(w_out, w_out_out)
         tails = buf[tails_at : tails_at + inner, :].astype(F32)
         for k in range(slots):
@@ -884,7 +911,7 @@
                     conv[k, :, LANES * q : LANES * (q + 1)] = buf[at : at + inner, :].astype(F32)
                 conv[k, :, LANES * whole :] = tails[:, tail * k : tail * (k + 1)]
             leave(conv.at[k], conv_out.at[k])
-        wide(w_in_t, w_in_at)
+        wide(w_in_t, w_in_at, places[1])
         leave(w_in_t, w_in_t_out)
         vec = sum(extra[at].astype(F32) for at in range(4))
         row = 0

time: 166 us -> 165 us (level)
    unnamed x38 -> x40, local copies, waits for them, and re-layouts: 5.34 us -> 4.51 us
where the time goes in v1:
time: 165 us; the launch traced here: 164 us
  Pallas kernels  68.9 us (42%)
  waiting for transfers between devices  50.5 us (31%)
  starting transfers between devices  25.3 us (15%)
  other arithmetic  11.1 us (7%)
  local copies, waits for them, and re-layouts  6.06 us (4%)
  between operations  1.86 us (1%)
    pallas_call x1, Pallas kernels, main_call(): pl.pallas_call(functools.partial(main_kernel, taps_of, groups), in_specs=...  36.8 us
    ppermute x10, waiting for transfers between devices, swap_dp(): return lax.ppermute(value, ('section', 'dp'), pairs)  27.5 us
    ppermute x6, waiting for transfers between devices, reduce_steps(): came.append(lax.ppermute(value, ('section', 'dp'), pairs))  15.9 us
    ppermute x10, starting transfers between devices, swap_dp(): return lax.ppermute(value, ('section', 'dp'), pairs)  14.5 us
    pallas_call x1, Pallas kernels, encoder_call(): pl.pallas_call(functools.partial(encoder_kernel, taps, groups), in_specs=...  14.2 us
    convert_element_type x12, other arithmetic, rounded_sum(): return total.astype(BF)  10.2 us
    pallas_call x1, Pallas kernels, first_call(): pl.pallas_call(functools.partial(first_kernel, block), in_specs=[ANY] * 3...  8.68 us
    ppermute x6, starting transfers between devices, reduce_steps(): came.append(lax.ppermute(value, ('section', 'dp'), pairs))  8.56 us
  transfers between devices with their start and end apart: 25, of which 15 were waited for; matrix products, arithmetic and copies ran while one was open for 6% of the time, Pallas kernels for 16%

profile of v1, /device:TPU:0, one launch (start us, length us, event | category | flops | bytes accessed | tf_op | source)
XLA Modules:
  0.0 163.9 jit_solution(4192520608663136897)
XLA Ops:
  0.6 0.5 collective-permute-start.2
  1.2 0.1 collective-permute-start
  1.2 0.4 collective-permute-start.1
  1.7 2.2 %pick_rows.1 = bf16[800,1024]{1,0:T(8,128)(2,1)} custom-call(bf16[2,800,1024]{2,1,0:T(8,128)(2,1)} %bitcast.27), custom_call_target="tpu_custom_call" | custom-call | bytes 8388608 | tf_op jit(solution)/shard_map/pick_rows/pallas_call | solution.py:459
  3.9 2.1 %collective-permute-done.refs_8_.got_in = bf16[400,800]{1,0:T(8,128)(2,1)S(1)} collective-permute-done((bf16[400,800]{1,0:T(8,128)(2,1)}, bf16[400,800]{1,0:T(8,128)(2,1)S(1)}, u32[]{:S(2)}, u32[]{:S(2)}) %collective-permute-start) | collective-permute-done | bytes 640032 | tf_op jit(solution)/shard_map/ppermute | solution.py:953
  6.0 1.0 collective-permute-done.1.refs_9_.got_out
  7.1 0.9 copy-done.18
  8.0 0.4 collective-permute-start.3
  9.0 1.4 pack_small.1.refs_3_.small_own
  10.4 0.1 collective-permute-start.4
  10.5 1.3 collective-permute-done.4.refs_4_.small_got
  11.8 0.6 copy-done.19
  12.4 1.2 copy-done.16
  13.5 36.8 %main_blocks.1 = (bf16[2,800,1024]{2,1,0:T(8,128)(2,1)}, bf16[800,1024]{1,0:T(8,128)(2,1)}, bf16[800,1024]{1,0:T(8,128)(2,1)}, bf16[4416,128]{1,0:T(8,128)(2,1)}...) custom-call(s32[2,8]{1,0:T(2,128)} %seq.1, ...), custom_call_target="tpu_custom_call" | custom-call | flops 39321600000 | bytes 62914560 | tf_op jit(solution)/shard_map/main_blocks/pallas_call | solution.py:638
  50.4 0.5 collective-permute-start.6
  50.9 2.6 %collective-permute-done.6 = bf16[4416,128]{1,0:T(8,128)(2,1)S(1)} collective-permute-done((bf16[4416,128]{1,0:T(8,128)(2,1)}, bf16[4416,128]{1,0:T(8,128)(2,1)S(1)}, u32[]{:S(2)}, u32[]{:S(2)}) %collective-permute-start.6) | collective-permute-done | bytes 1130528 | tf_op jit(solution)/shard_map/ppermute | solution.py:953
  53.5 2.4 %add_convert_fusion.1 = bf16[2208,128]{1,0:T(8,128)(2,1)} fusion(bf16[4416,128]{1,0:T(8,128)(2,1)S(1)} %collective-permute-done.6, bf16[4416,128]{1,0:T(8,128)(2,1)} %get-tuple-element.59), kind=kLoop, calls=%fused_computation.3 | loop fusion | flops 1130496 | bytes 1695744 | tf_op jit(solution)/shard_map/convert_element_type | solution.py:966
  55.9 2.7 %collective-permute-start.7 = (bf16[2208,128]{1,0:T(8,128)(2,1)}, bf16[2208,128]{1,0:T(8,128)(2,1)S(1)}, u32[]{:S(2)}, u32[]{:S(2)}) collective-permute-start(bf16[2208,128]{1,0:T(8,128)(2,1)} %add_convert_fusion.1), channel_id=1, source_target_pairs={{0,1},{1,0},{2,3},{3,2},{4,5},{5,4},{6,7},{7,6},{8,9},{9,8},{10,11... | collective-permute-start | bytes 1695752 | tf_op jit(solution)/shard_map/ppermute | solution.py:959
  58.6 14.2 %encoder_back.1 = (bf16[400,1024]{1,0:T(8,128)(2,1)}, f32[8,800]{1,0:T(8,128)}, bf16[5824,128]{1,0:T(8,128)(2,1)}, bf16[5824,128]{1,0:T(8,128)(2,1)}) custom-call(s32[2,8]{1,0:T(2,128)} %seq.1, bf16[800,1024]{1,0:T(8,128)(2,1)} %get-tuple-element.61.gy_in.gy_first.gy_second, f32[8,800]{1,0:T(8,128)} %pack_small.1.refs_3_.small_own, f32[8,800]{1,0:T(8,128)} %copy-done.19, ...), custom_call_target="tpu_custom_call" | custom-call | flops 20971520000 | bytes 20971520 | tf_op jit(solution)/shard_map/encoder_back/pallas_call | solution.py:742
  72.9 0.2 collective-permute-start.9
  73.1 1.2 add_convert_fusion.9
  74.4 1.6 collective-permute-start.11
  75.9 5.2 %collective-permute-done.11 = bf16[1152,128]{1,0:T(8,128)(2,1)S(1)} collective-permute-done((bf16[1152,128]{1,0:T(8,128)(2,1)S(1)}, bf16[1152,128]{1,0:T(8,128)(2,1)S(1)}, u32[]{:S(2)}, u32[]{:S(2)}) %collective-permute-start.11) | collective-permute-done | bytes 294944 | tf_op jit(solution)/shard_map/ppermute | solution.py:959
  81.2 1.3 add_convert_fusion.8
  82.4 0.7 pad_maximum_fusion.5
  83.2 1.6 collective-permute-start.12
  84.7 1.2 add_convert_fusion
  86.0 0.2 copy-done.3
  86.1 1.5 collective-permute-start.10
  87.6 8.7 %first_0.1 = (bf16[2,800,1024]{2,1,0:T(8,128)(2,1)}, bf16[800,1024]{1,0:T(8,128)(2,1)}, bf16[48,128]{1,0:T(8,128)(2,1)}) custom-call(bf16[800,1024]{1,0:T(8,128)(2,1)} %get-tuple-element.61.gy_in.gy_first.gy_second, bf16[800,1024]{1,0:T(8,128)(2,1)} %get-tuple-element.61.gy_in.gy_first.gy_second, bf16[400,1024]{1,0:T(8,128)(2,1)} %get-tuple-element.72.grad_projected_in, ...), custom_call_target="tpu_custom_call" | custom-call | flops 5242880000 | bytes 20971520 | tf_op jit(solution)/shard_map/first_0/pallas_call | solution.py:812
  96.3 1.0 add_convert_fusion.7
  97.4 0.6 collective-permute-done.10
  98.0 1.4 add_convert_fusion.5
  99.4 1.6 collective-permute-start.13
  101.0 1.3 bitcast_dynamic-update-slice_fusion.1
  102.3 0.7 copy-done.15
  103.0 2.6 %collective-permute-start.15 = (bf16[1152,128]{1,0:T(8,128)(2,1)S(1)}, bf16[1152,128]{1,0:T(8,128)(2,1)S(1)}, u32[]{:S(2)}, u32[]{:S(2)}) collective-permute-start(bf16[1152,128]{1,0:T(8,128)(2,1)S(1)} %add_convert_fusion.7), channel_id=1, source_target_pairs={{0,8},{1,9},{2,10},{3,11},{4,12},{5,13},{6,14},{7,15},{8,0},{9,1},... | collective-permute-start | bytes 884744 | tf_op jit(solution)/shard_map/ppermute | solution.py:959
  105.6 1.6 collective-permute-done.13
  107.2 1.4 add_convert_fusion.4
  108.6 0.5 collective-permute-start.14
  109.2 8.7 %collective-permute-done.15 = bf16[1152,128]{1,0:T(8,128)(2,1)S(1)} collective-permute-done((bf16[1152,128]{1,0:T(8,128)(2,1)S(1)}, bf16[1152,128]{1,0:T(8,128)(2,1)S(1)}, u32[]{:S(2)}, u32[]{:S(2)}) %collective-permute-start.15) | collective-permute-done | bytes 294944 | tf_op jit(solution)/shard_map/ppermute | solution.py:959
  117.9 0.1 add_convert_fusion.6
  118.0 0.5 collective-permute-start.17
  118.5 2.1 %collective-permute-done.14 = bf16[1504,128]{1,0:T(8,128)(2,1)S(1)} collective-permute-done((bf16[1504,128]{1,0:T(8,128)(2,1)S(1)}, bf16[1504,128]{1,0:T(8,128)(2,1)S(1)}, u32[]{:S(2)}, u32[]{:S(2)}) %collective-permute-start.14) | collective-permute-done | bytes 385056 | tf_op jit(solution)/shard_map/ppermute | solution.py:959
  120.6 0.1 add_convert_fusion.3
  120.7 2.0 %collective-permute-start.16 = (bf16[1504,128]{1,0:T(8,128)(2,1)S(1)}, bf16[1504,128]{1,0:T(8,128)(2,1)S(1)}, u32[]{:S(2)}, u32[]{:S(2)}) collective-permute-start(bf16[1504,128]{1,0:T(8,128)(2,1)S(1)} %add_convert_fusion.3), channel_id=1, source_target_pairs={{0,8},{1,9},{2,10},{3,11},{4,12},{5,13},{6,14},{7,15},{8,0},{9,1},... | collective-permute-start | bytes 1155080 | tf_op jit(solution)/shard_map/ppermute | solution.py:959
  122.7 0.2 bitcast_dynamic-update-slice_fusion
  122.9 1.8 %collective-permute-done.17 = bf16[1104,128]{1,0:T(8,128)(2,1)S(1)} collective-permute-done((bf16[1104,128]{1,0:T(8,128)(2,1)S(1)}, bf16[1104,128]{1,0:T(8,128)(2,1)S(1)}, u32[]{:S(2)}, u32[]{:S(2)}) %collective-permute-start.17) | collective-permute-done | bytes 282656 | tf_op jit(solution)/shard_map/ppermute | solution.py:959
  124.7 0.7 collective-permute-start.19
  125.4 1.3 collective-permute-start.20
  126.7 2.0 %collective-permute-start.21 = (bf16[2256,128]{1,0:T(8,128)(2,1)S(1)}, bf16[2256,128]{1,0:T(8,128)(2,1)S(1)}, u32[]{:S(2)}, u32[]{:S(2)}) collective-permute-start(bf16[2256,128]{1,0:T(8,128)(2,1)S(1)} %pad_maximum_fusion.1.refs_4_), channel_id=1, source_target_pairs={{0,17},{1,16},{2,19},{3,18},{4,21},{5,20},{6,23},{7,22},{8,25},{9,... | collective-permute-start | bytes 1732616 | tf_op jit(solution)/shard_map/ppermute | solution.py:1017
  128.8 4.7 %collective-permute-done.16 = bf16[1504,128]{1,0:T(8,128)(2,1)S(1)} collective-permute-done((bf16[1504,128]{1,0:T(8,128)(2,1)S(1)}, bf16[1504,128]{1,0:T(8,128)(2,1)S(1)}, u32[]{:S(2)}, u32[]{:S(2)}) %collective-permute-start.16) | collective-permute-done | bytes 385056 | tf_op jit(solution)/shard_map/ppermute | solution.py:959
  133.4 0.1 add_convert_fusion.2
  133.6 0.1 collective-permute-start.18
  133.7 4.6 %collective-permute-done.21.refs_7_ = bf16[2256,128]{1,0:T(8,128)(2,1)S(1)} collective-permute-done((bf16[2256,128]{1,0:T(8,128)(2,1)S(1)}, bf16[2256,128]{1,0:T(8,128)(2,1)S(1)}, u32[]{:S(2)}, u32[]{:S(2)}) %collective-permute-start.21) | collective-permute-done | bytes 577568 | tf_op jit(solution)/shard_map/ppermute | solution.py:1017
  138.4 2.8 %collective-permute-done.18 = bf16[1456,128]{1,0:T(8,128)(2,1)S(1)} collective-permute-done((bf16[1456,128]{1,0:T(8,128)(2,1)S(1)}, bf16[1456,128]{1,0:T(8,128)(2,1)S(1)}, u32[]{:S(2)}, u32[]{:S(2)}) %collective-permute-start.18) | collective-permute-done | bytes 372768 | tf_op jit(solution)/shard_map/ppermute | solution.py:959
  141.2 0.1 pad_maximum_fusion.refs_0_
  141.3 1.9 %collective-permute-start.22 = (bf16[2960,128]{1,0:T(8,128)(2,1)S(1)}, bf16[2960,128]{1,0:T(8,128)(2,1)S(1)}, u32[]{:S(2)}, u32[]{:S(2)}) collective-permute-start(bf16[2960,128]{1,0:T(8,128)(2,1)S(1)} %pad_maximum_fusion.refs_0_), channel_id=1, source_target_pairs={{0,1},{1,0},{2,3},{3,2},{4,5},{5,4},{6,7},{7,6},{8,9},{9,8},{10,11... | collective-permute-start | bytes 2273288 | tf_op jit(solution)/shard_map/ppermute | solution.py:1017
  143.2 1.3 collective-permute-start.23
  144.5 1.3 collective-permute-start.24
  145.8 9.0 %collective-permute-done.22.refs_1_ = bf16[2960,128]{1,0:T(8,128)(2,1)S(1)} collective-permute-done((bf16[2960,128]{1,0:T(8,128)(2,1)S(1)}, bf16[2960,128]{1,0:T(8,128)(2,1)S(1)}, u32[]{:S(2)}, u32[]{:S(2)}) %collective-permute-start.22) | collective-permute-done | bytes 757792 | tf_op jit(solution)/shard_map/ppermute | solution.py:1017
  154.9 0.9 copy-done.6
  155.8 2.2 %collective-permute-done.24.refs_3_ = bf16[2960,128]{1,0:T(8,128)(2,1)} collective-permute-done((bf16[2960,128]{1,0:T(8,128)(2,1)S(1)}, bf16[2960,128]{1,0:T(8,128)(2,1)}, u32[]{:S(2)}, u32[]{:S(2)}) %collective-permute-start.24) | collective-permute-done | bytes 757792 | tf_op jit(solution)/shard_map/ppermute | solution.py:1017
  158.0 5.6 %unpack.1 = (f32[400,800]{1,0:T(8,128)}, f32[400,800]{1,0:T(8,128)}, f32[5,400,400]{2,1,0:T(8,128)}, f32[1,800]{1,0:T(1,128)}, f32[1,800]{1,0:T(1,128)}, /*index...) custom-call(bf16[2960,128]{1,0:T(8,128)(2,1)} %copy-done, bf16[2960,128]{1,0:T(8,128)(2,1)} %copy-done.5, ...), custom_call_target="tpu_custom_call" | custom-call | tf_op jit(solution)/shard_map/unpack/pallas_call | solution.py:933
  (56 shorter events, 0.3 us)
Async XLA Ops:
  0.6 7.3 %collective-permute-start.2 = (bf16[5,400,400]{2,1,0:T(8,128)(2,1)}, bf16[5,400,400]{2,1,0:T(8,128)(2,1)}, u32[]{:S(2)}, u32[]{:S(2)}) collective-permute-start(bf16[5,400,400]{2,1,0:T(8,128)(2,1)} %bitcast.34), channel_id=1, source_target_pairs={{0,16},{16,0},{1,17},{17,1},{2,18},{18,2},{3,19},{19,3},{4,20},{20... | collective-permute-start | bytes 4800008 | tf_op jit(solution)/shard_map/ppermute | solution.py:953
  1.2 4.9 %collective-permute-start = (bf16[400,800]{1,0:T(8,128)(2,1)}, bf16[400,800]{1,0:T(8,128)(2,1)S(1)}, u32[]{:S(2)}, u32[]{:S(2)}) collective-permute-start(bf16[400,800]{1,0:T(8,128)(2,1)} %bitcast.42), channel_id=1, source_target_pairs={{0,16},{16,0},{1,17},{17,1},{2,18},{18,2},{3,19},{19,3},{4,20},{20... | collective-permute-start | bytes 1920008 | tf_op jit(solution)/shard_map/ppermute | solution.py:953
  1.2 5.8 %collective-permute-start.1 = (bf16[400,800]{1,0:T(8,128)(2,1)}, bf16[400,800]{1,0:T(8,128)(2,1)S(1)}, u32[]{:S(2)}, u32[]{:S(2)}) collective-permute-start(bf16[400,800]{1,0:T(8,128)(2,1)} %bitcast.39), channel_id=1, source_target_pairs={{0,16},{16,0},{1,17},{17,1},{2,18},{18,2},{3,19},{19,3},{4,20},{20... | collective-permute-start | bytes 1920008 | tf_op jit(solution)/shard_map/ppermute | solution.py:953
  6.0 1.0 copy-start.17
  7.1 0.9 copy-start.18
  8.0 3.8 %collective-permute-start.3 = (bf16[800,1024]{1,0:T(8,128)(2,1)}, bf16[800,1024]{1,0:T(8,128)(2,1)S(1)}, u32[]{:S(2)}, u32[]{:S(2)}) collective-permute-start(bf16[800,1024]{1,0:T(8,128)(2,1)} %pick_rows.1), channel_id=1, source_target_pairs={{0,16},{16,0},{1,17},{17,1},{2,18},{18,2},{3,19},{19,3},{4,20},{20... | collective-permute-start | bytes 4915208 | tf_op jit(solution)/shard_map/ppermute | solution.py:953
  10.4 1.4 collective-permute-start.4
  11.8 0.6 copy-start.19
  12.4 1.2 copy-start.16
  50.4 3.2 %collective-permute-start.6 = (bf16[4416,128]{1,0:T(8,128)(2,1)}, bf16[4416,128]{1,0:T(8,128)(2,1)S(1)}, u32[]{:S(2)}, u32[]{:S(2)}) collective-permute-start(bf16[4416,128]{1,0:T(8,128)(2,1)} %get-tuple-element.60), channel_id=1, source_target_pairs={{0,16},{16,0},{1,17},{17,1},{2,18},{18,2},{3,19},{19,3},{4,20},{20... | collective-permute-start | bytes 3391496 | tf_op jit(solution)/shard_map/ppermute | solution.py:953
  53.5 19.5 %copy-start.4 = (bf16[4416,128]{1,0:T(8,128)(2,1)}, bf16[4416,128]{1,0:T(8,128)(2,1)S(1)}, u32[]{:S(2)}) copy-start(bf16[4416,128]{1,0:T(8,128)(2,1)S(1)} %collective-permute-done.6) | copy-start | bytes 3391492
  55.9 17.1 %collective-permute-start.7 = (bf16[2208,128]{1,0:T(8,128)(2,1)}, bf16[2208,128]{1,0:T(8,128)(2,1)S(1)}, u32[]{:S(2)}, u32[]{:S(2)}) collective-permute-start(bf16[2208,128]{1,0:T(8,128)(2,1)} %add_convert_fusion.1), channel_id=1, source_target_pairs={{0,1},{1,0},{2,3},{3,2},{4,5},{5,4},{6,7},{7,6},{8,9},{9,8},{10,11... | collective-permute-start | bytes 1695752 | tf_op jit(solution)/shard_map/ppermute | solution.py:959
  58.6 15.7 %copy-start.12 = (bf16[48,128]{1,0:T(8,128)(2,1)S(1)}, bf16[48,128]{1,0:T(8,128)(2,1)}, u32[]{:S(2)}) copy-start(bf16[48,128]{1,0:T(8,128)(2,1)} %get-tuple-element.71) | copy-start | bytes 36868
  72.9 11.9 %collective-permute-start.9 = (bf16[5824,128]{1,0:T(8,128)(2,1)}, bf16[5824,128]{1,0:T(8,128)(2,1)S(1)}, u32[]{:S(2)}, u32[]{:S(2)}) collective-permute-start(bf16[5824,128]{1,0:T(8,128)(2,1)} %get-tuple-element.79), channel_id=1, source_target_pairs={{0,16},{16,0},{1,17},{17,1},{2,18},{18,2},{3,19},{19,3},{4,20},{20... | collective-permute-start | bytes 4472840 | tf_op jit(solution)/shard_map/ppermute | solution.py:953
  73.1 2.8 %copy-start.10 = (bf16[2208,128]{1,0:T(8,128)(2,1)}, bf16[2208,128]{1,0:T(8,128)(2,1)S(1)}, u32[]{:S(2)}) copy-start(bf16[2208,128]{1,0:T(8,128)(2,1)S(1)} %collective-permute-done.7) | copy-start | bytes 1695748
  74.3 10.4 %copy-start.2 = (bf16[5824,128]{1,0:T(8,128)(2,1)S(1)}, bf16[5824,128]{1,0:T(8,128)(2,1)}, u32[]{:S(2)}) copy-start(bf16[5824,128]{1,0:T(8,128)(2,1)} %get-tuple-element.78) | copy-start | bytes 4472836
  74.4 6.8 %collective-permute-start.11 = (bf16[1152,128]{1,0:T(8,128)(2,1)S(1)}, bf16[1152,128]{1,0:T(8,128)(2,1)S(1)}, u32[]{:S(2)}, u32[]{:S(2)}) collective-permute-start(bf16[1152,128]{1,0:T(8,128)(2,1)S(1)} %pad_maximum_fusion.4), channel_id=1, source_target_pairs={{0,2},{1,3},{2,0},{3,1},{4,6},{5,7},{6,4},{7,5},{8,10},{9,11},{10,... | collective-permute-start | bytes 884744 | tf_op jit(solution)/shard_map/ppermute | solution.py:959
  75.9 25.1 %collective-permute-start.5 = (bf16[800,1024]{1,0:T(8,128)(2,1)}, bf16[800,1024]{1,0:T(8,128)(2,1)S(1)}, u32[]{:S(2)}, u32[]{:S(2)}) collective-permute-start(bf16[800,1024]{1,0:T(8,128)(2,1)} %get-tuple-element.57), channel_id=1, source_target_pairs={{0,16},{16,0},{1,17},{17,1},{2,18},{18,2},{3,19},{19,3},{4,20},{20... | collective-permute-start | bytes 4915208 | tf_op jit(solution)/shard_map/ppermute | solution.py:953
  83.2 13.1 %collective-permute-start.12 = (bf16[1152,128]{1,0:T(8,128)(2,1)}, bf16[1152,128]{1,0:T(8,128)(2,1)}, u32[]{:S(2)}, u32[]{:S(2)}) collective-permute-start(bf16[1152,128]{1,0:T(8,128)(2,1)} %pad_maximum_fusion.5), channel_id=1, source_target_pairs={{0,4},{1,5},{2,6},{3,7},{4,0},{5,1},{6,2},{7,3},{8,12},{9,13},{10,... | collective-permute-start | bytes 884744 | tf_op jit(solution)/shard_map/ppermute | solution.py:959
  84.7 1.4 copy-start.3
  86.1 11.9 %collective-permute-start.10 = (bf16[2912,128]{1,0:T(8,128)(2,1)}, bf16[2912,128]{1,0:T(8,128)(2,1)}, u32[]{:S(2)}, u32[]{:S(2)}) collective-permute-start(bf16[2912,128]{1,0:T(8,128)(2,1)} %add_convert_fusion), channel_id=1, source_target_pairs={{0,1},{1,0},{2,3},{3,2},{4,5},{5,4},{6,7},{7,6},{8,9},{9,8},{10,11... | collective-permute-start | bytes 2236424 | tf_op jit(solution)/shard_map/ppermute | solution.py:959
  96.3 3.1 %copy-start.11 = (bf16[48,128]{1,0:T(8,128)(2,1)S(1)}, bf16[48,128]{1,0:T(8,128)(2,1)}, u32[]{:S(2)}) copy-start(bf16[48,128]{1,0:T(8,128)(2,1)} %get-tuple-element.82) | copy-start | bytes 36868
  99.4 7.8 %collective-permute-start.13 = (bf16[1504,128]{1,0:T(8,128)(2,1)S(1)}, bf16[1504,128]{1,0:T(8,128)(2,1)S(1)}, u32[]{:S(2)}, u32[]{:S(2)}) collective-permute-start(bf16[1504,128]{1,0:T(8,128)(2,1)S(1)} %pad_maximum_fusion.2), channel_id=1, source_target_pairs={{0,2},{1,3},{2,0},{3,1},{4,6},{5,7},{6,4},{7,5},{8,10},{9,11},{10,... | collective-permute-start | bytes 1155080 | tf_op jit(solution)/shard_map/ppermute | solution.py:959
  101.0 2.0 %copy-start.15 = (bf16[800,1024]{1,0:T(8,128)(2,1)S(1)}, bf16[800,1024]{1,0:T(8,128)(2,1)}, u32[]{:S(2)}) copy-start(bf16[800,1024]{1,0:T(8,128)(2,1)} %get-tuple-element.77) | copy-start | bytes 4915204
  103.0 19.7 %collective-permute-start.8 = (bf16[800,1024]{1,0:T(8,128)(2,1)S(1)}, bf16[800,1024]{1,0:T(8,128)(2,1)S(1)}, u32[]{:S(2)}, u32[]{:S(2)}) collective-permute-start(bf16[800,1024]{1,0:T(8,128)(2,1)S(1)} %copy-done.15), channel_id=1, source_target_pairs={{0,16},{16,0},{1,17},{17,1},{2,18},{18,2},{3,19},{19,3},{4,20},{20... | collective-permute-start | bytes 4915208 | tf_op jit(solution)/shard_map/ppermute | solution.py:953
  103.0 14.9 %collective-permute-start.15 = (bf16[1152,128]{1,0:T(8,128)(2,1)S(1)}, bf16[1152,128]{1,0:T(8,128)(2,1)S(1)}, u32[]{:S(2)}, u32[]{:S(2)}) collective-permute-start(bf16[1152,128]{1,0:T(8,128)(2,1)S(1)} %add_convert_fusion.7), channel_id=1, source_target_pairs={{0,8},{1,9},{2,10},{3,11},{4,12},{5,13},{6,14},{7,15},{8,0},{9,1},... | collective-permute-start | bytes 884744 | tf_op jit(solution)/shard_map/ppermute | solution.py:959
  108.6 14.1 %copy-start.13 = (bf16[2,800,1024]{2,1,0:T(8,128)(2,1)S(1)}, bf16[2,800,1024]{2,1,0:T(8,128)(2,1)}, u32[]{:S(2)}) copy-start(bf16[2,800,1024]{2,1,0:T(8,128)(2,1)} %get-tuple-element.76) | copy-start | bytes 9830404
  108.6 11.9 %collective-permute-start.14 = (bf16[1504,128]{1,0:T(8,128)(2,1)S(1)}, bf16[1504,128]{1,0:T(8,128)(2,1)S(1)}, u32[]{:S(2)}, u32[]{:S(2)}) collective-permute-start(bf16[1504,128]{1,0:T(8,128)(2,1)S(1)} %pad_maximum_fusion.3), channel_id=1, source_target_pairs={{0,4},{1,5},{2,6},{3,7},{4,0},{5,1},{6,2},{7,3},{8,12},{9,13},{10,... | collective-permute-start | bytes 1155080 | tf_op jit(solution)/shard_map/ppermute | solution.py:959
  118.0 6.7 %collective-permute-start.17 = (bf16[1104,128]{1,0:T(8,128)(2,1)S(1)}, bf16[1104,128]{1,0:T(8,128)(2,1)S(1)}, u32[]{:S(2)}, u32[]{:S(2)}) collective-permute-start(bf16[1104,128]{1,0:T(8,128)(2,1)S(1)} %slice.124), channel_id=1, source_target_pairs={{0,2},{1,3},{2,0},{3,1},{4,6},{5,7},{6,4},{7,5},{8,10},{9,11},{10,... | collective-permute-start | bytes 847880 | tf_op jit(solution)/shard_map/ppermute | solution.py:959
  120.7 12.8 %collective-permute-start.16 = (bf16[1504,128]{1,0:T(8,128)(2,1)S(1)}, bf16[1504,128]{1,0:T(8,128)(2,1)S(1)}, u32[]{:S(2)}, u32[]{:S(2)}) collective-permute-start(bf16[1504,128]{1,0:T(8,128)(2,1)S(1)} %add_convert_fusion.3), channel_id=1, source_target_pairs={{0,8},{1,9},{2,10},{3,11},{4,12},{5,13},{6,14},{7,15},{8,0},{9,1},... | collective-permute-start | bytes 1155080 | tf_op jit(solution)/shard_map/ppermute | solution.py:959
  122.9 32.0 %copy-start.14 = (bf16[2,800,1024]{2,1,0:T(8,128)(2,1)}, bf16[2,800,1024]{2,1,0:T(8,128)(2,1)S(1)}, u32[]{:S(2)}) copy-start(bf16[2,800,1024]{2,1,0:T(8,128)(2,1)S(1)} %bitcast_dynamic-update-slice_fusion) | copy-start | bytes 9830404
  124.7 16.6 %copy-start.1 = (bf16[2256,128]{1,0:T(8,128)(2,1)}, bf16[2256,128]{1,0:T(8,128)(2,1)S(1)}, u32[]{:S(2)}) copy-start(bf16[2256,128]{1,0:T(8,128)(2,1)S(1)} %pad_maximum_fusion.1.refs_4_) | copy-start | bytes 1732612
  124.7 9.0 %collective-permute-start.19 = (bf16[2256,128]{1,0:T(8,128)(2,1)S(1)}, bf16[2256,128]{1,0:T(8,128)(2,1)S(1)}, u32[]{:S(2)}, u32[]{:S(2)}) collective-permute-start(bf16[2256,128]{1,0:T(8,128)(2,1)S(1)} %pad_maximum_fusion.1.refs_4_), channel_id=1, source_target_pairs={{16,18},{17,19},{18,16},{19,17},{20,22},{21,23},{22,20},{23,21},{2... | collective-permute-start | bytes 1732616 | tf_op jit(solution)/shard_map/ppermute | solution.py:1017
  125.4 8.3 %collective-permute-start.20 = (bf16[2256,128]{1,0:T(8,128)(2,1)S(1)}, bf16[2256,128]{1,0:T(8,128)(2,1)S(1)}, u32[]{:S(2)}, u32[]{:S(2)}) collective-permute-start(bf16[2256,128]{1,0:T(8,128)(2,1)S(1)} %pad_maximum_fusion.1.refs_4_), channel_id=1, source_target_pairs={{0,16},{1,17},{2,18},{3,19},{4,20},{5,21},{6,22},{7,23},{8,24},{9,... | collective-permute-start | bytes 1732616 | tf_op jit(solution)/shard_map/ppermute | solution.py:1017
  126.7 11.6 %collective-permute-start.21 = (bf16[2256,128]{1,0:T(8,128)(2,1)S(1)}, bf16[2256,128]{1,0:T(8,128)(2,1)S(1)}, u32[]{:S(2)}, u32[]{:S(2)}) collective-permute-start(bf16[2256,128]{1,0:T(8,128)(2,1)S(1)} %pad_maximum_fusion.1.refs_4_), channel_id=1, source_target_pairs={{0,17},{1,16},{2,19},{3,18},{4,21},{5,20},{6,23},{7,22},{8,25},{9,... | collective-permute-start | bytes 1732616 | tf_op jit(solution)/shard_map/ppermute | solution.py:1017
  133.6 7.6 %collective-permute-start.18 = (bf16[1456,128]{1,0:T(8,128)(2,1)S(1)}, bf16[1456,128]{1,0:T(8,128)(2,1)S(1)}, u32[]{:S(2)}, u32[]{:S(2)}) collective-permute-start(bf16[1456,128]{1,0:T(8,128)(2,1)S(1)} %slice.126), channel_id=1, source_target_pairs={{0,2},{1,3},{2,0},{3,1},{4,6},{5,7},{6,4},{7,5},{8,10},{9,11},{10,... | collective-permute-start | bytes 1118216 | tf_op jit(solution)/shard_map/ppermute | solution.py:959
  133.7 21.2 %copy-start.7 = (bf16[2256,128]{1,0:T(8,128)(2,1)}, bf16[2256,128]{1,0:T(8,128)(2,1)S(1)}, u32[]{:S(2)}) copy-start(bf16[2256,128]{1,0:T(8,128)(2,1)S(1)} %collective-permute-done.19.refs_5_) | copy-start | bytes 1732612
  133.7 21.2 %copy-start.8 = (bf16[2256,128]{1,0:T(8,128)(2,1)}, bf16[2256,128]{1,0:T(8,128)(2,1)S(1)}, u32[]{:S(2)}) copy-start(bf16[2256,128]{1,0:T(8,128)(2,1)S(1)} %collective-permute-done.20.refs_6_) | copy-start | bytes 1732612
  138.4 16.5 %copy-start.9 = (bf16[2256,128]{1,0:T(8,128)(2,1)}, bf16[2256,128]{1,0:T(8,128)(2,1)S(1)}, u32[]{:S(2)}) copy-start(bf16[2256,128]{1,0:T(8,128)(2,1)S(1)} %collective-permute-done.21.refs_7_) | copy-start | bytes 1732612
  141.3 16.8 %copy-start = (bf16[2960,128]{1,0:T(8,128)(2,1)}, bf16[2960,128]{1,0:T(8,128)(2,1)S(1)}, u32[]{:S(2)}) copy-start(bf16[2960,128]{1,0:T(8,128)(2,1)S(1)} %pad_maximum_fusion.refs_0_) | copy-start | bytes 2273284
  141.3 13.6 %collective-permute-start.22 = (bf16[2960,128]{1,0:T(8,128)(2,1)S(1)}, bf16[2960,128]{1,0:T(8,128)(2,1)S(1)}, u32[]{:S(2)}, u32[]{:S(2)}) collective-permute-start(bf16[2960,128]{1,0:T(8,128)(2,1)S(1)} %pad_maximum_fusion.refs_0_), channel_id=1, source_target_pairs={{0,1},{1,0},{2,3},{3,2},{4,5},{5,4},{6,7},{7,6},{8,9},{9,8},{10,11... | collective-permute-start | bytes 2273288 | tf_op jit(solution)/shard_map/ppermute | solution.py:1017
  143.2 11.7 %collective-permute-start.23 = (bf16[2960,128]{1,0:T(8,128)(2,1)S(1)}, bf16[2960,128]{1,0:T(8,128)(2,1)S(1)}, u32[]{:S(2)}, u32[]{:S(2)}) collective-permute-start(bf16[2960,128]{1,0:T(8,128)(2,1)S(1)} %pad_maximum_fusion.refs_0_), channel_id=1, source_target_pairs={{16,0},{17,1},{18,2},{19,3},{20,4},{21,5},{22,6},{23,7},{24,8},{25... | collective-permute-start | bytes 2273288 | tf_op jit(solution)/shard_map/ppermute | solution.py:1017
  144.5 13.5 %collective-permute-start.24 = (bf16[2960,128]{1,0:T(8,128)(2,1)S(1)}, bf16[2960,128]{1,0:T(8,128)(2,1)}, u32[]{:S(2)}, u32[]{:S(2)}) collective-permute-start(bf16[2960,128]{1,0:T(8,128)(2,1)S(1)} %pad_maximum_fusion.refs_0_), channel_id=1, source_target_pairs={{16,2},{17,3},{18,0},{19,1},{20,6},{21,7},{22,4},{23,5},{24,10},{2... | collective-permute-start | bytes 2273288 | tf_op jit(solution)/shard_map/ppermute | solution.py:1017
  154.9 3.2 %copy-start.5 = (bf16[2960,128]{1,0:T(8,128)(2,1)}, bf16[2960,128]{1,0:T(8,128)(2,1)S(1)}, u32[]{:S(2)}) copy-start(bf16[2960,128]{1,0:T(8,128)(2,1)S(1)} %collective-permute-done.22.refs_1_) | copy-start | bytes 2273284
  154.9 0.9 copy-start.6
